TPU v7x, 128 devices: a whole 4x4x4 slice. The times are simulated.
128 devices in a mesh: gx: 4 (over z), gy: 4 (over y), gz: 8 (over x, core).
Axes of the slice: x: 4, y: 4, z: 4, core: 2. Of those that a mesh axis runs over, the one named last changes fastest.
Arguments:
- old_state: float32 [16, 32, 64, 1024], P(None, 'gx', 'gy', 'gz'), may hold values from -12 to 12
- remap_weights: bfloat16 [16384, 4, 128, 128], P(('gx', 'gy', 'gz')), may hold values from -0.176776695 to 0.609375
- new_owner: int32 [16384, 1], P(('gx', 'gy', 'gz')), may hold values from 0 to 127; in each aligned block of 128 rows (0 to 127, 128 to 255, ...) at most 2 rows name the same one
- new_block: int32 [16384], P(('gx', 'gy', 'gz')), may hold values from 0 to 127
Outputs:
- new_state: float32 [16, 32, 64, 1024], P(None, 'gx', 'gy', 'gz')
Inputs may be any that keep to these rules, and one draw needn't show every extreme that they name: `new_owner`: A device is numbered in mesh order, gx slowest and gz fastest. The 128 rows of one device name any one device at most 2 times.
All inputs are finite; a program needn't handle non-finite values.
Results may differ from a plain program's by a relative error of at most 0.0003.
The roundings to bfloat16 on the way count: a program that leaves them out, or rounds other values in their place, can miss the bound.
Values sent between devices are 32-bit elements; how exact they have to be, the bound alone decides.
A program may use at most 64 MiB of HBM per device.

v0:
```python
import jax
import jax.numpy as jnp
from jax import lax
from jax.sharding import PartitionSpec as P


def padded_2(array, sides, width):
    for axis, dim in sides:
        devices, length = (lax.axis_size(axis), array.shape[dim])
        up = [(i, (i + 1) % devices) for i in range(devices - 1)]
        down = [(j, i) for i, j in up]
        last = lax.slice_in_dim(array, length - width, length, axis=dim)
        first = lax.slice_in_dim(array, 0, width, axis=dim)
        before = lax.ppermute(last, axis, up)
        after = lax.ppermute(first, axis, down)
        array = jnp.concatenate([before, array, after], axis=dim)
    return array


def shifted(values, dimension, low_cut, high_cut):
    return lax.slice_in_dim(values, low_cut, values.shape[dimension] - high_cut, axis=dimension)


def trimmed(values, dimensions):
    for dimension in dimensions:
        values = shifted(values, dimension, 1, 1)
    return values


def limited(padded):
    center = trimmed(padded, (1, 2, 3))
    slopes = []
    for dimension in (1, 2, 3):
        remaining = tuple((entry for entry in (1, 2, 3) if entry != dimension))
        strip_cells = trimmed(padded, remaining)
        below_step = center - shifted(strip_cells, dimension, 0, 2)
        above_step = shifted(strip_cells, dimension, 2, 0) - center
        slopes.append(
            0.5
            * (jnp.sign(below_step) + jnp.sign(above_step))
            * jnp.minimum(jnp.abs(below_step), jnp.abs(above_step))
        )
    return jnp.stack([center] + slopes)


def smooth(values, dimension):
    return (
        shifted(values, dimension, 0, 2)
        + 2.0 * shifted(values, dimension, 1, 1)
        + shifted(values, dimension, 2, 0)
    )


def spread(values, dimension):
    return shifted(values, dimension, 2, 0) - shifted(values, dimension, 0, 2)


def wave_speed(fields):
    velocity_sq = fields[1] * fields[1] + fields[2] * fields[2] + fields[3] * fields[3]
    return jnp.sqrt(1.0 + 0.05 * (fields[4] * fields[4] + velocity_sq))


def lagrange_step(fields, padded_rim, speed_max):
    pressure = padded_rim[0]
    grad_x = spread(smooth(smooth(pressure, 1), 2), 0) / 32.0
    grad_y = spread(smooth(smooth(pressure, 0), 2), 1) / 32.0
    grad_z = spread(smooth(smooth(pressure, 0), 1), 2) / 32.0
    divergence = (
        spread(smooth(smooth(padded_rim[1], 1), 2), 0)
        + spread(smooth(smooth(padded_rim[2], 0), 2), 1)
        + spread(smooth(smooth(padded_rim[3], 0), 1), 2)
    ) / 32.0
    time_step = 0.5 / speed_max
    new_pressure = fields[0] - time_step * divergence
    new_velocity = fields[1:4] - time_step * jnp.stack([grad_x, grad_y, grad_z])
    new_energy = fields[4] - time_step * fields[0] * divergence
    return jnp.concatenate([new_pressure[None], new_velocity, new_energy[None], fields[5:]], axis=0)


def on_device(old_state, remap_weights, new_owner, new_block):
    fields_count, cells_x, cells_y, cells_z = old_state.shape
    local_blocks = cells_x * cells_y
    padded = padded_2(old_state, (("gx", 1), ("gy", 2), ("gz", 3)), 1)
    moments = limited(padded).astype(jnp.bfloat16).reshape(4, fields_count, local_blocks, cells_z)
    contributions = jnp.einsum(
        "kfbi,bkij->bfj", moments, remap_weights, preferred_element_type=jnp.float32
    )
    count_x = lax.axis_size("gx")
    count_y = lax.axis_size("gy")
    count_z = lax.axis_size("gz")
    devices_total = count_x * count_y * count_z
    capacity = max(2, 2 * local_blocks // devices_total)
    slots_total = devices_total * capacity
    owners = new_owner[:, 0]
    onehot = (owners[:, None] == jnp.arange(devices_total, dtype=jnp.int32)[None, :]).astype(
        jnp.int32
    )
    earlier = jnp.cumsum(onehot, axis=0) - onehot
    slot_index = jnp.sum(earlier * onehot, axis=1)
    positions = owners * capacity + slot_index
    outgoing = (
        jnp.zeros((slots_total, fields_count, cells_z), jnp.float32)
        .at[positions]
        .set(contributions)
    )
    target_ids = jnp.full((slots_total,), -1, jnp.int32).at[positions].set(new_block)
    arrived, arrived_ids = (
        lax.all_to_all(outgoing, ("gx", "gy", "gz"), split_axis=0, concat_axis=0, tiled=True),
        lax.all_to_all(target_ids, ("gx", "gy", "gz"), split_axis=0, concat_axis=0, tiled=True),
    )
    segment_ids = jnp.where(arrived_ids >= 0, arrived_ids, local_blocks)
    blocks = jax.ops.segment_sum(arrived, segment_ids, num_segments=local_blocks + 1)[:local_blocks]
    fields = blocks.reshape(cells_x, cells_y, fields_count, cells_z).transpose(2, 0, 1, 3)
    fields_rim = padded_2(fields[0:4], (("gx", 1), ("gy", 2), ("gz", 3)), 1)
    speed_max = lax.pmax(jnp.max(wave_speed(fields)), ("gx", "gy", "gz"))
    return lagrange_step(fields, fields_rim, speed_max)


def solution(mesh):
    return jax.shard_map(
        on_device,
        mesh=mesh,
        in_specs=(
            P(None, "gx", "gy", "gz"),
            P(("gx", "gy", "gz"), None, None, None),
            P(("gx", "gy", "gz"), None),
            P(("gx", "gy", "gz")),
        ),
        out_specs=P(None, "gx", "gy", "gz"),
        check_vma=False,
    )
```

profile of v0, /device:TPU:1, one launch (start us, length us, event | category | flops | bytes accessed | tf_op | source)
XLA Modules:
  0.0 224.9 jit_solution(11691729204106161905)
XLA Ops:
  0.0 1.9 copy.18
  1.9 0.7 fusion.56
  2.6 4.4 %collective-permute-start = (f32[16,1,16,128]{3,0,2,1:T(8,128)S(1)}, f32[16,1,16,128]{3,0,2,1:T(8,128)S(1)}, u32[]{:S(2)}, u32[]{:S(2)}) collective-permute-start(f32[16,1,16,128]{3,0,2,1:T(8,128)S(1)} %get-tuple-element.16), channel_id=1, source_target_pairs={{0,32},{32,64},{64,96},{1,33},{33,65},{65,97},{2,34},{34,66},{66,9... | collective-permute-start | bytes 393224 | tf_op jit(solution)/shard_map/ppermute | solution.py:14
  7.0 1.3 collective-permute-start.1
  8.7 0.4 collective-permute-done
  9.2 0.6 constant_dynamic-update-slice_fusion.1
  9.8 3.9 %collective-permute-done.1 = f32[16,1,16,128]{3,0,2,1:T(8,128)} collective-permute-done((f32[16,1,16,128]{3,0,2,1:T(8,128)}, f32[16,1,16,128]{3,0,2,1:T(8,128)}, u32[]{:S(2)}, u32[]{:S(2)}) %collective-permute-start.1) | collective-permute-done | bytes 131104 | tf_op jit(solution)/shard_map/ppermute | solution.py:15
  13.6 0.9 constant_dynamic-update-slice_fusion
  14.5 0.7 fusion.54
  15.2 3.8 %collective-permute-start.2 = (f32[16,10,1,128]{3,0,2,1:T(8,128)}, f32[16,10,1,128]{3,0,2,1:T(8,128)}, u32[]{:S(2)}, u32[]{:S(2)}) collective-permute-start(f32[16,10,1,128]{3,0,2,1:T(8,128)} %get-tuple-element.11), channel_id=1, source_target_pairs={{0,8},{8,16},{16,24},{1,9},{9,17},{17,25},{2,10},{10,18},{18,26},{... | collective-permute-start | bytes 245768 | tf_op jit(solution)/shard_map/ppermute | solution.py:14
  19.1 1.3 collective-permute-start.3
  20.4 1.1 scatter_custom_fusion
  21.5 0.8 all_to_all.11
  22.3 12.6 %all-to-all-start = ((s32[128,2,1]{1,2,0:T(1,128)}), s32[128,2,1]{1,2,0:T(1,128)}, u32[]{:S(2)}, u32[]{:S(2)}) async-start(s32[128,2,1]{1,2,0:T(1,128)} %bitcast.78), calls=%async_computation | async-start | bytes 131072 | tf_op jit(solution)/shard_map/all_to_all | solution.py:109
  35.0 1.1 copy.15
  36.1 1.1 pad_maximum_fusion
  37.2 2.1 fusion.53
  39.3 3.0 %copy.25 = f32[16,10,18,1]{2,0,3,1:T(8,128)} copy(f32[16,10,18,1]{3,0,2,1:T(8,128)} %get-tuple-element.9) | data formatting | bytes 23040 | tf_op jit(solution)/shard_map/slice | solution.py:12
  42.4 3.5 %collective-permute-start.4 = (f32[16,10,18,1]{2,0,3,1:T(8,128)}, f32[16,10,18,1]{2,0,3,1:T(8,128)}, u32[]{:S(2)}, u32[]{:S(2)}) collective-permute-start(f32[16,10,18,1]{2,0,3,1:T(8,128)} %copy.25), channel_id=1, source_target_pairs={{0,1},{1,2},{2,3},{3,4},{4,5},{5,6},{6,7},{8,9},{9,10},{10,11},{11... | collective-permute-start | bytes 34568 | tf_op jit(solution)/shard_map/ppermute | solution.py:14
  45.9 3.0 %copy.28 = f32[16,10,18,1]{2,0,3,1:T(8,128)} copy(f32[16,10,18,1]{3,0,2,1:T(8,128)} %get-tuple-element.10) | data formatting | bytes 23040 | tf_op jit(solution)/shard_map/slice | solution.py:13
  48.9 2.1 collective-permute-start.5
  51.0 2.2 multiply_convert_fusion.2
  53.3 3.1 %copy.26 = f32[16,10,18,1]{3,0,2,1:T(8,128)} copy(f32[16,10,18,1]{2,0,3,1:T(8,128)} %collective-permute-done.4) | data formatting | bytes 23040 | tf_op jit(solution)/shard_map/ppermute | solution.py:14
  56.3 3.0 %copy.29 = f32[16,10,18,1]{3,0,2,1:T(8,128)} copy(f32[16,10,18,1]{2,0,3,1:T(8,128)} %collective-permute-done.5) | data formatting | bytes 23040 | tf_op jit(solution)/shard_map/ppermute | solution.py:15
  59.4 3.8 %multiply_convert_fusion.1 = (bf16[16,8,16,128]{3,0,2,1:T(8,128)(2,1)S(1)}, bf16[16,8,16,128]{3,0,2,1:T(8,128)(2,1)S(1)}) fusion(f32[16,10,1,128]{3,0,2,1:T(8,128)} %collective-permute-done.3, f32[16,10,16,128]{3,0,2,1:T(8,128)S(1)} %constant_dynamic-update-slice_fusion, f32[16,10,1,128]{3,0,2,1:T(8,128)} %collective-permute-done.2, ...), kind=kLoop, calls=%fused_computation.32 | loop fusion | flops 7864320 | bytes 3594752 | tf_op jit(solution)/shard_map/convert.5
  63.2 7.0 %fusion.8 = f32[128,16,128]{2,1,0:T(8,128)S(1)} fusion(bf16[128,4,128,128]{3,2,1,0:T(8,128)(2,1)} %param.5, bf16[1,16,128,128]{3,1,0,2:T(8,128)(2,1)S(1)} %bitcast.76, bf16[1,16,128,128]{3,1,0,2:T(8,128)(2,1)S(1)} %bitcast.75, bf16[1,16,128,128]{3,1,0,2:T(8,128)(2,1)S(1)} %bitcast.74, bf16[1,16,128,128]{3,1,0,2:T(8,128)(2,1)S(1)} %bitcast.77), kind=kOutput, calls=%fused_computation.12 | convolution fusion | flops 271581184 | bytes 19922944 | tf_op jit(solution)/shard_map/kfbi,bkij->bfj/dot_general | solution.py:85
  70.2 1.5 broadcast_in_dim.26
  71.7 13.7 %scatter_fusion = f32[256,16,128]{2,1,0:T(8,128)} fusion(f32[256,16,128]{2,1,0:T(8,128)} %broadcast_in_dim.26, s32[128]{0:T(128)S(1)} %fusion.48, f32[128,16,128]{2,1,0:T(8,128)S(1)} %fusion.8), kind=kCustom, calls=%fused_computation.1 | custom fusion | bytes 3146240 | tf_op jit(solution)/shard_map/scatter | solution.py:104
  85.4 9.9 %all-to-all-start.1 = ((f32[256,16,128]{2,1,0:T(8,128)}), f32[256,16,128]{2,1,0:T(8,128)S(1)}, u32[]{:S(2)}, u32[]{:S(2)}) async-start(f32[256,16,128]{2,1,0:T(8,128)} %scatter_fusion), calls=%async_computation.1 | async-start | bytes 4194304 | tf_op jit(solution)/shard_map/all_to_all | solution.py:108
  95.2 0.5 broadcast.90
  95.7 1.6 reduce.3
  97.5 28.2 %all-to-all-done.1 = f32[256,16,128]{2,1,0:T(8,128)S(1)} async-done(((f32[256,16,128]{2,1,0:T(8,128)}), f32[256,16,128]{2,1,0:T(8,128)S(1)}, u32[]{:S(2)}, u32[]{:S(2)}) %all-to-all-start.1) | async-done | bytes 2097184 | tf_op jit(solution)/shard_map/all_to_all | solution.py:108
  125.8 8.9 %scatter_fusion.1 = f32[129,16,128]{2,1,0:T(8,128)S(1)} fusion(f32[129,16,128]{2,1,0:T(8,128)S(1)} %broadcast_in_dim.23, s32[256]{0:T(256)S(1)} %bitcast.79, f32[256,16,128]{2,1,0:T(8,128)S(1)} %all-to-all-done.1), kind=kCustom, calls=%fused_computation.2 | custom fusion | flops 524288 | bytes 6292480 | tf_op jit(solution)/shard_map/scatter-add | solution.py:112
  134.8 0.3 copy.37
  135.2 1.7 collective-permute-start.6
  136.9 1.3 collective-permute-start.7
  138.2 3.3 %collective-permute-done.7 = f32[4,1,16,128]{3,2,1,0:T(8,128)S(1)} collective-permute-done((f32[4,1,16,128]{3,2,1,0:T(8,128)S(1)}, f32[4,1,16,128]{3,2,1,0:T(8,128)S(1)}, u32[]{:S(2)}, u32[]{:S(2)}) %collective-permute-start.7) | collective-permute-done | bytes 32800 | tf_op jit(solution)/shard_map/ppermute | solution.py:15
  141.6 2.3 %collective-permute-start.8 = (f32[4,10,1,128]{3,2,1,0:T(1,128)S(1)}, f32[4,10,1,128]{3,2,1,0:T(1,128)S(1)}, u32[]{:S(2)}, u32[]{:S(2)}) collective-permute-start(f32[4,10,1,128]{3,2,1,0:T(1,128)S(1)} %get-tuple-element.24), channel_id=1, source_target_pairs={{0,8},{8,16},{16,24},{1,9},{9,17},{17,25},{2,10},{10,18},{18,26},{... | collective-permute-start | bytes 61448 | tf_op jit(solution)/shard_map/ppermute | solution.py:14
  143.9 1.3 collective-permute-start.9
  145.2 3.2 %collective-permute-done.9 = f32[4,10,1,128]{3,2,1,0:T(1,128)S(1)} collective-permute-done((f32[4,10,1,128]{3,2,1,0:T(1,128)S(1)}, f32[4,10,1,128]{3,2,1,0:T(1,128)S(1)}, u32[]{:S(2)}, u32[]{:S(2)}) %collective-permute-start.9) | collective-permute-done | bytes 20512 | tf_op jit(solution)/shard_map/ppermute | solution.py:15
  148.4 0.6 copy-done.5
  149.1 1.0 fusion.57
  150.1 5.2 %collective-permute-start.10 = (f32[4,10,18,1]{3,2,1,0:T(8,128)}, f32[4,10,18,1]{3,2,1,0:T(8,128)S(1)}, u32[]{:S(2)}, u32[]{:S(2)}) collective-permute-start(f32[4,10,18,1]{3,2,1,0:T(8,128)} %get-tuple-element.22), channel_id=1, source_target_pairs={{0,1},{1,2},{2,3},{3,4},{4,5},{5,6},{6,7},{8,9},{9,10},{10,11},{11... | collective-permute-start | bytes 8648 | tf_op jit(solution)/shard_map/ppermute | solution.py:14
  155.3 2.3 %collective-permute-start.11 = (f32[4,10,18,1]{3,2,1,0:T(8,128)S(1)}, f32[4,10,18,1]{3,2,1,0:T(8,128)S(1)}, u32[]{:S(2)}, u32[]{:S(2)}) collective-permute-start(f32[4,10,18,1]{3,2,1,0:T(8,128)S(1)} %get-tuple-element.23), channel_id=1, source_target_pairs={{1,0},{2,1},{3,2},{4,3},{5,4},{6,5},{7,6},{9,8},{10,9},{11,10},{12... | collective-permute-start | bytes 8648 | tf_op jit(solution)/shard_map/ppermute | solution.py:15
  157.6 0.7 fusion.43
  158.3 62.3 %pmax.7 = f32[]{:T(128)} all-reduce(f32[]{:T(128)} %fusion.43), channel_id=1, replica_groups=mesh['gx'=4,'gy'=4,'gz'=8] {'gx','gy','gz'}, use_global_device_ids=true, to_apply=%region_6.7 | all-reduce | flops 1 | bytes 8 | tf_op jit(solution)/shard_map/pmax | solution.py:115
  221.4 1.4 pad_maximum_fusion.12
  223.8 1.1 pad_maximum_fusion.11
  (51 shorter events, 1.9 us)
Async XLA Ops:
  0.0 9.1 %copy-start = (f32[16,8,16,128]{3,2,1,0:T(8,128)S(1)}, f32[16,8,16,128]{3,2,1,0:T(8,128)}, u32[]{:S(2)}) copy-start(f32[16,8,16,128]{3,2,1,0:T(8,128)} %param.4) | copy-start | bytes 3145732
  0.0 8.3 %copy-start.6 = (s32[128,1]{0,1:T(1,128)S(1)}, s32[128,1]{0,1:T(1,128)}, u32[]{:S(2)}) copy-start(s32[128,1]{0,1:T(1,128)} %param.6) | copy-start | bytes 1540
  2.6 6.5 %collective-permute-start = (f32[16,1,16,128]{3,0,2,1:T(8,128)S(1)}, f32[16,1,16,128]{3,0,2,1:T(8,128)S(1)}, u32[]{:S(2)}, u32[]{:S(2)}) collective-permute-start(f32[16,1,16,128]{3,0,2,1:T(8,128)S(1)} %get-tuple-element.16), channel_id=1, source_target_pairs={{0,32},{32,64},{64,96},{1,33},{33,65},{65,97},{2,34},{34,66},{66,9... | collective-permute-start | bytes 393224 | tf_op jit(solution)/shard_map/ppermute | solution.py:14
  7.0 6.6 %collective-permute-start.1 = (f32[16,1,16,128]{3,0,2,1:T(8,128)}, f32[16,1,16,128]{3,0,2,1:T(8,128)}, u32[]{:S(2)}, u32[]{:S(2)}) collective-permute-start(f32[16,1,16,128]{3,0,2,1:T(8,128)} %get-tuple-element.15), channel_id=1, source_target_pairs={{32,0},{64,32},{96,64},{33,1},{65,33},{97,65},{34,2},{66,34},{98,6... | collective-permute-start | bytes 393224 | tf_op jit(solution)/shard_map/ppermute | solution.py:15
  15.2 20.9 %collective-permute-start.2 = (f32[16,10,1,128]{3,0,2,1:T(8,128)}, f32[16,10,1,128]{3,0,2,1:T(8,128)}, u32[]{:S(2)}, u32[]{:S(2)}) collective-permute-start(f32[16,10,1,128]{3,0,2,1:T(8,128)} %get-tuple-element.11), channel_id=1, source_target_pairs={{0,8},{8,16},{16,24},{1,9},{9,17},{17,25},{2,10},{10,18},{18,26},{... | collective-permute-start | bytes 245768 | tf_op jit(solution)/shard_map/ppermute | solution.py:14
  19.1 17.1 %collective-permute-start.3 = (f32[16,10,1,128]{3,0,2,1:T(8,128)}, f32[16,10,1,128]{3,0,2,1:T(8,128)}, u32[]{:S(2)}, u32[]{:S(2)}) collective-permute-start(f32[16,10,1,128]{3,0,2,1:T(8,128)} %get-tuple-element.12), channel_id=1, source_target_pairs={{8,0},{16,8},{24,16},{9,1},{17,9},{25,17},{10,2},{18,10},{26,18},{... | collective-permute-start | bytes 245768 | tf_op jit(solution)/shard_map/ppermute | solution.py:15
  22.3 63.1 %all-to-all-start = ((s32[128,2,1]{1,2,0:T(1,128)}), s32[128,2,1]{1,2,0:T(1,128)}, u32[]{:S(2)}, u32[]{:S(2)}) async-start(s32[128,2,1]{1,2,0:T(1,128)} %bitcast.78), calls=%async_computation | async-start | bytes 131072 | tf_op jit(solution)/shard_map/all_to_all | solution.py:109
  42.4 10.9 %collective-permute-start.4 = (f32[16,10,18,1]{2,0,3,1:T(8,128)}, f32[16,10,18,1]{2,0,3,1:T(8,128)}, u32[]{:S(2)}, u32[]{:S(2)}) collective-permute-start(f32[16,10,18,1]{2,0,3,1:T(8,128)} %copy.25), channel_id=1, source_target_pairs={{0,1},{1,2},{2,3},{3,4},{4,5},{5,6},{6,7},{8,9},{9,10},{10,11},{11... | collective-permute-start | bytes 34568 | tf_op jit(solution)/shard_map/ppermute | solution.py:14
  48.9 7.4 %collective-permute-start.5 = (f32[16,10,18,1]{2,0,3,1:T(8,128)}, f32[16,10,18,1]{2,0,3,1:T(8,128)}, u32[]{:S(2)}, u32[]{:S(2)}) collective-permute-start(f32[16,10,18,1]{2,0,3,1:T(8,128)} %copy.28), channel_id=1, source_target_pairs={{1,0},{2,1},{3,2},{4,3},{5,4},{6,5},{7,6},{9,8},{10,9},{11,10},{12... | collective-permute-start | bytes 34568 | tf_op jit(solution)/shard_map/ppermute | solution.py:15
  59.4 3.8 %copy-start.1 = (bf16[16,8,16,128]{3,0,2,1:T(8,128)(2,1)S(1)}, bf16[16,8,16,128]{3,0,2,1:T(8,128)(2,1)}, u32[]{:S(2)}) copy-start(bf16[16,8,16,128]{3,0,2,1:T(8,128)(2,1)} %multiply_convert_fusion.2) | copy-start | bytes 1572868
  59.4 3.8 %copy-start.2 = (bf16[16,8,16,128]{3,0,2,1:T(8,128)(2,1)S(1)}, bf16[16,8,16,128]{3,0,2,1:T(8,128)(2,1)}, u32[]{:S(2)}) copy-start(bf16[16,8,16,128]{3,0,2,1:T(8,128)(2,1)} %copy.15) | copy-start | bytes 1572868
  85.4 40.4 %all-to-all-start.1 = ((f32[256,16,128]{2,1,0:T(8,128)}), f32[256,16,128]{2,1,0:T(8,128)S(1)}, u32[]{:S(2)}, u32[]{:S(2)}) async-start(f32[256,16,128]{2,1,0:T(8,128)} %scatter_fusion), calls=%async_computation.1 | async-start | bytes 4194304 | tf_op jit(solution)/shard_map/all_to_all | solution.py:108
  135.2 3.0 %collective-permute-start.6 = (f32[4,1,16,128]{3,2,1,0:T(8,128)S(1)}, f32[4,1,16,128]{3,2,1,0:T(8,128)S(1)}, u32[]{:S(2)}, u32[]{:S(2)}) collective-permute-start(f32[4,1,16,128]{3,2,1,0:T(8,128)S(1)} %get-tuple-element.13), channel_id=1, source_target_pairs={{0,32},{32,64},{64,96},{1,33},{33,65},{65,97},{2,34},{34,66},{66,9... | collective-permute-start | bytes 98312 | tf_op jit(solution)/shard_map/ppermute | solution.py:14
  136.9 4.7 %collective-permute-start.7 = (f32[4,1,16,128]{3,2,1,0:T(8,128)S(1)}, f32[4,1,16,128]{3,2,1,0:T(8,128)S(1)}, u32[]{:S(2)}, u32[]{:S(2)}) collective-permute-start(f32[4,1,16,128]{3,2,1,0:T(8,128)S(1)} %get-tuple-element.14), channel_id=1, source_target_pairs={{32,0},{64,32},{96,64},{33,1},{65,33},{97,65},{34,2},{66,34},{98,6... | collective-permute-start | bytes 98312 | tf_op jit(solution)/shard_map/ppermute | solution.py:15
  141.5 6.9 %copy-start.3 = (f32[4,1,16,128]{3,2,1,0:T(8,128)}, f32[4,1,16,128]{3,2,1,0:T(8,128)S(1)}, u32[]{:S(2)}) copy-start(f32[4,1,16,128]{3,2,1,0:T(8,128)S(1)} %collective-permute-done.7) | copy-start | bytes 98308
  141.6 3.6 %collective-permute-start.8 = (f32[4,10,1,128]{3,2,1,0:T(1,128)S(1)}, f32[4,10,1,128]{3,2,1,0:T(1,128)S(1)}, u32[]{:S(2)}, u32[]{:S(2)}) collective-permute-start(f32[4,10,1,128]{3,2,1,0:T(1,128)S(1)} %get-tuple-element.24), channel_id=1, source_target_pairs={{0,8},{8,16},{16,24},{1,9},{9,17},{17,25},{2,10},{10,18},{18,26},{... | collective-permute-start | bytes 61448 | tf_op jit(solution)/shard_map/ppermute | solution.py:14
  143.9 4.5 %collective-permute-start.9 = (f32[4,10,1,128]{3,2,1,0:T(1,128)S(1)}, f32[4,10,1,128]{3,2,1,0:T(1,128)S(1)}, u32[]{:S(2)}, u32[]{:S(2)}) collective-permute-start(f32[4,10,1,128]{3,2,1,0:T(1,128)S(1)} %get-tuple-element.25), channel_id=1, source_target_pairs={{8,0},{16,8},{24,16},{9,1},{17,9},{25,17},{10,2},{18,10},{26,18},{... | collective-permute-start | bytes 61448 | tf_op jit(solution)/shard_map/ppermute | solution.py:15
  145.2 3.2 %copy-start.4 = (f32[4,10,1,128]{3,2,1,0:T(1,128)}, f32[4,10,1,128]{3,2,1,0:T(1,128)S(1)}, u32[]{:S(2)}) copy-start(f32[4,10,1,128]{3,2,1,0:T(1,128)S(1)} %collective-permute-done.8) | copy-start | bytes 61444
  148.4 0.6 copy-start.5
  150.1 71.3 %collective-permute-start.10 = (f32[4,10,18,1]{3,2,1,0:T(8,128)}, f32[4,10,18,1]{3,2,1,0:T(8,128)S(1)}, u32[]{:S(2)}, u32[]{:S(2)}) collective-permute-start(f32[4,10,18,1]{3,2,1,0:T(8,128)} %get-tuple-element.22), channel_id=1, source_target_pairs={{0,1},{1,2},{2,3},{3,4},{4,5},{5,6},{6,7},{8,9},{9,10},{10,11},{11... | collective-permute-start | bytes 8648 | tf_op jit(solution)/shard_map/ppermute | solution.py:14
  155.3 66.1 %collective-permute-start.11 = (f32[4,10,18,1]{3,2,1,0:T(8,128)S(1)}, f32[4,10,18,1]{3,2,1,0:T(8,128)S(1)}, u32[]{:S(2)}, u32[]{:S(2)}) collective-permute-start(f32[4,10,18,1]{3,2,1,0:T(8,128)S(1)} %get-tuple-element.23), channel_id=1, source_target_pairs={{1,0},{2,1},{3,2},{4,3},{5,4},{6,5},{7,6},{9,8},{10,9},{11,10},{12... | collective-permute-start | bytes 8648 | tf_op jit(solution)/shard_map/ppermute | solution.py:15
where the time goes:
time: 226 us; the launch traced here: 225 us
  blocking collectives  62.3 us (28%)
  starting transfers between devices  53 us (23%)
  local copies, waits for them, and re-layouts  40.2 us (18%)
  waiting for transfers between devices  39 us (17%)
  other arithmetic  22.3 us (10%)
  matrix products  7.02 us (3%)
    pmax x1, blocking collectives, on_device(): speed_max = lax.pmax(jnp.max(wave_speed(fields)), ('gx', 'gy', 'gz'))  62.3 us
    all_to_all x1, waiting for transfers between devices, on_device(): lax.all_to_all(outgoing, ('gx', 'gy', 'gz'), split_axis=0, concat_axis=0,...  28.2 us
    ppermute x6, starting transfers between devices, padded_2(): before = lax.ppermute(last, axis, up)  21 us
    scatter x1, local copies, waits for them, and re-layouts, on_device(): outgoing = jnp.zeros((slots_total, fields_count, cells_z), jnp.float32).a...  13.7 us
    all_to_all x1, starting transfers between devices, on_device(): lax.all_to_all(target_ids, ('gx', 'gy', 'gz'), split_axis=0, concat_axis=...  12.6 us
    ppermute x6, waiting for transfers between devices, padded_2(): after = lax.ppermute(first, axis, down)  10.4 us
    all_to_all x1, starting transfers between devices, on_device(): lax.all_to_all(outgoing, ('gx', 'gy', 'gz'), split_axis=0, concat_axis=0,...  9.86 us
    ppermute x6, starting transfers between devices, padded_2(): after = lax.ppermute(first, axis, down)  9.5 us
  transfers between devices with their start and end apart: 14, of which 5 were waited for; matrix products, arithmetic and copies ran while one was open for 22% of the time, Pallas kernels for 0%

commit v1 on v0

v1 whole, which is shorter than its diff:
```python
import jax
import jax.numpy as jnp
from jax import lax
from jax.experimental import pallas as pl
from jax.experimental.pallas import tpu as pltpu
from jax.sharding import PartitionSpec as P

MESH = pl.DeviceIdType.MESH
F32 = jnp.float32
BF16 = jnp.bfloat16
CHUNKS = 4
STEPS = 128 // CHUNKS


def four(j):
    return (2 + j * (j + 1) // 2) % 4


def eight(j):
    return (4 + ((j + 1) // 2) * (2 * (j % 2) - 1) + 8) % 8


def offsets(i):
    return four(i % 4), four((i // 4 + i + 1) % 4), eight((i // 16 + i // 4 + i + 2) % 8)


def limit(below, above):
    return jnp.maximum(jnp.minimum(below, above), 0.0) + jnp.minimum(jnp.maximum(below, above), 0.0)


def kernel(
    state, weights, owner, block, out,
    w, nat, pad, zsend, zrecv, contrib, sendbuf, recvbuf, meta, metat, slotv, slots, lhs, rhs, fields, rim,
    xrecv, ysend, yrecv, erecv, zcol, zcolr, max1, max2,
    w_sem, in_sem, slot_sem, out_sem, halo_s, halo_r, m1_s, m1_r, m2_s, m2_r, a2a_s, a2a_r, rim_s, rim_r,
    x1_s, x1_r, x2_s, x2_r,
):
    gx, gy, gz = lax.axis_index("gx"), lax.axis_index("gy"), lax.axis_index("gz")
    plane = gx * 4 + gy
    me = plane * 8 + gz

    def at(a, b, c):
        return ((gx + a + 4) % 4, (gy + b + 4) % 4, (gz + c + 8) % 8)

    def remote(src, dst, send, recv, device):
        return pltpu.make_async_remote_copy(
            src_ref=src, dst_ref=dst, send_sem=send, recv_sem=recv, device_id=device, device_id_type=MESH
        )

    load_state = pltpu.make_async_copy(state, nat, in_sem.at[0])
    load_state.start()

    def load_weights(x):
        return pltpu.make_async_copy(weights.at[pl.ds(x * 16, 16)], w.at[pl.ds(x * 16, 16)], w_sem.at[x])

    for x in (1, 2, 3, 4, 5, 6, 0, 7):
        load_weights(x).start()
    barrier = pltpu.get_barrier_semaphore()

    def greet(t, carry):
        pl.semaphore_signal(
            barrier, inc=1, device_id=((gx + t // 32) % 4, (gy + (t // 8) % 4) % 4, (gz + t % 8) % 8),
            device_id_type=MESH,
        )
        return carry

    lax.fori_loop(1, 128, greet, 0)

    lane = lax.broadcasted_iota(jnp.int32, (128, 128), 1)
    sub = lax.broadcasted_iota(jnp.int32, (128, 128), 0)
    named = jnp.broadcast_to(owner[...], (128, 128)).T == lane
    first = jnp.min(jnp.where(named, sub, 128), axis=0, keepdims=True)
    last = jnp.max(jnp.where(named, sub, -1), axis=0, keepdims=True)
    slotv[...] = jnp.concatenate([first, jnp.where(last > first, last, 128)] * 4, axis=0)
    fetch_slots = pltpu.make_async_copy(slotv, slots, slot_sem.at[0])
    fetch_slots.start()
    meta[plane, gz] = jnp.concatenate([owner[...], block[...]], axis=0)
    contrib[128] = jnp.zeros((16, 128), F32)

    load_state.wait()
    lane16 = lax.broadcasted_iota(jnp.int32, (16, 128), 1)

    def to_blocks(x, carry):
        low, high = carry
        for part in range(2):
            for half in range(2):
                tile = nat[pl.ds(half * 8, 8), x, pl.ds(part * 8, 8), :]
                pad[x + 1, pl.ds(1 + part * 8, 8), pl.ds(half * 8, 8), :] = jnp.swapaxes(tile, 0, 1)
        for y in range(16):
            b = x * 16 + y
            rolled = pltpu.roll(pad[x + 1, y + 1], b, 1)
            low = jnp.where(lane16 == b, rolled, low)
            high = jnp.where(lane16 == (b + 127) % 128, rolled, high)
        return low, high

    zeros = jnp.zeros((16, 128), F32)
    low, high = lax.fori_loop(0, 8, to_blocks, (zeros, zeros))
    zsend[0] = low
    zsend[1] = pltpu.roll(high, 1, 1)
    pl.semaphore_wait(barrier, 127)

    z_up = remote(zsend.at[1], zrecv.at[0], halo_s.at[0], halo_r.at[0], at(0, 0, 1))
    z_down = remote(zsend.at[0], zrecv.at[1], halo_s.at[1], halo_r.at[1], at(0, 0, -1))
    inner = pl.ds(1, 16)
    cells = pl.ds(1, 8)
    x_up = remote(pad.at[8, inner], pad.at[0, inner], halo_s.at[2], halo_r.at[2], at(1, 0, 0))
    x_down = remote(pad.at[1, inner], pad.at[9, inner], halo_s.at[3], halo_r.at[3], at(-1, 0, 0))
    y_up = remote(pad.at[cells, 16], pad.at[cells, 0], halo_s.at[4], halo_r.at[4], at(0, 1, 0))
    y_down = remote(pad.at[cells, 1], pad.at[cells, 17], halo_s.at[5], halo_r.at[5], at(0, -1, 0))
    for copy in (z_up, z_down, x_up, x_down, y_up, y_down):
        copy.start()

    def meta_one(c):
        mine = meta.at[plane, gz]
        return remote(mine, mine, m1_s.at[c], m1_r.at[c], (gx, gy, (gz + c) % 8))

    def meta_two(e):
        to = (plane + e) % 16
        return remote(meta.at[plane], meta.at[plane], m2_s.at[e], m2_r.at[e], (to // 4, to % 4, gz))

    def start_all(make, lo, hi):
        def body(i, carry):
            make(i).start()
            return carry
        lax.fori_loop(lo, hi, body, 0)

    def recv_all(make, lo, hi):
        def body(i, carry):
            make(i).wait_recv()
            return carry
        lax.fori_loop(lo, hi, body, 0)

    def sent_all(make, lo, hi):
        def body(i, carry):
            make(i).wait_send()
            return carry
        lax.fori_loop(lo, hi, body, 0)

    start_all(meta_one, 1, 8)

    z_up.wait_recv()
    z_down.wait_recv()
    z_low = jnp.where(gz == 0, 0.0, zrecv[0])
    z_high = jnp.where(gz == 7, 0.0, zrecv[1])

    def contribute(x, y):
        b = (x - 1) * 16 + (y - 1)
        q = pad[x, y]
        before = jnp.where(lane16 == 0, pltpu.roll(z_low, (128 - b) % 128, 1), pltpu.roll(q, 1, 1))
        after = jnp.where(lane16 == 127, pltpu.roll(z_high, 127 - b, 1), pltpu.roll(q, 127, 1))
        moments = jnp.concatenate(
            [
                q,
                limit(q - pad[x - 1, y], pad[x + 1, y] - q),
                limit(q - pad[x, y - 1], pad[x, y + 1] - q),
                limit(q - before, after - q),
            ],
            axis=1,
        ).astype(BF16)
        contrib[b] = jnp.dot(moments, w[b], preferred_element_type=F32)

    def inner_plane(x, carry):
        load_weights(x - 1).wait()
        for y in range(2, 16):
            contribute(x, y)
        return carry

    lax.fori_loop(2, 8, inner_plane, 0)
    recv_all(meta_one, 1, 8)
    start_all(meta_two, 1, 16)
    for copy in (x_up, x_down, y_up, y_down):
        copy.wait_recv()

    @pl.when(gx == 0)
    def _():
        pad[0, 1:17] = jnp.zeros((16, 16, 128), F32)

    @pl.when(gx == 3)
    def _():
        pad[9, 1:17] = jnp.zeros((16, 16, 128), F32)

    @pl.when(gy == 0)
    def _():
        pad[1:9, 0] = jnp.zeros((8, 16, 128), F32)

    @pl.when(gy == 3)
    def _():
        pad[1:9, 17] = jnp.zeros((8, 16, 128), F32)

    def side_columns(x, carry):
        contribute(x, 1)
        contribute(x, 16)
        return carry

    lax.fori_loop(2, 8, side_columns, 0)
    load_weights(0).wait()
    load_weights(7).wait()

    def side_planes(side, carry):
        for y in range(1, 17):
            contribute(1 + side * 7, y)
        return carry

    lax.fori_loop(0, 2, side_planes, 0)
    fetch_slots.wait()

    def delivery(i):
        a, b, c = offsets(i)
        return remote(sendbuf.at[i], recvbuf.at[i], a2a_s.at[i], a2a_r.at[i], at(a, b, c))

    def deliver(i, carry):
        a, b, c = offsets(i)
        x, y, z = at(a, b, c)
        to = x * 32 + y * 8 + z
        for slot in range(2):
            sendbuf[i, slot] = contrib[jnp.clip(slots[slot, to], 0, 128)]
        delivery(i).start()
        return carry

    lax.fori_loop(0, 127, deliver, 0)
    for slot in range(2):
        recvbuf[127, slot] = contrib[jnp.clip(slots[slot, me], 0, 128)]

    recv_all(meta_two, 1, 16)

    def in_order(i, carry):
        a, b, c = offsets(i)
        x, y, z = at(-a, -b, -c)
        row = meta[x * 4 + y, z]
        metat[0, pl.ds(i, 1), :] = row[0:1]
        metat[1, pl.ds(i, 1), :] = row[1:2]
        return carry

    lax.fori_loop(0, 128, in_order, 0)
    mine = metat[0] == me
    target = metat[1].astype(F32)
    lane = lane.astype(F32)
    first = jnp.min(jnp.where(mine, lane, 128.0), axis=1, keepdims=True)
    last = jnp.max(jnp.where(mine, lane, -1.0), axis=1, keepdims=True)
    target_0 = jnp.max(jnp.where(mine & (lane == first), target, -1.0), axis=1, keepdims=True)
    target_1 = jnp.max(jnp.where(mine & (lane == last) & (last > first), target, -1.0), axis=1, keepdims=True)
    hot_0 = jnp.where(target_0 == lane, 1.0, 0.0)
    hot_1 = jnp.where(target_1 == lane, 1.0, 0.0)
    for chunk in range(CHUNKS):
        rows = slice(chunk * STEPS, (chunk + 1) * STEPS)
        both = jnp.concatenate([hot_0[rows], hot_1[rows], hot_0[rows], hot_1[rows]], axis=0)
        lhs[chunk] = both.T.astype(BF16)

    for chunk in range(CHUNKS):
        recv_all(delivery, chunk * STEPS, min((chunk + 1) * STEPS, 127))
        for part in range(STEPS // 16):
            for slot in range(2):
                for half in range(2):
                    tile = recvbuf[pl.ds(chunk * STEPS + part * 16, 16), slot, pl.ds(half * 8, 8), :]
                    tile = jnp.swapaxes(tile, 0, 1)
                    upper = tile.astype(BF16)
                    lower = (tile - upper.astype(F32)).astype(BF16)
                    row = slot * STEPS + part * 16
                    rhs[pl.ds(half * 8, 8), pl.ds(row, 16), :] = upper
                    rhs[pl.ds(half * 8, 8), pl.ds(2 * STEPS + row, 16), :] = lower

        def accumulate(f, carry):
            part_sum = jnp.dot(lhs[chunk], rhs[f], preferred_element_type=F32)
            fields[f] = part_sum if chunk == 0 else fields[f] + part_sum
            return carry

        lax.fori_loop(0, 16, accumulate, 0)

    square = fields[4] * fields[4] + (fields[1] * fields[1] + fields[2] * fields[2] + fields[3] * fields[3])
    max1[gz] = jnp.max(square.reshape(16, 8, 128), axis=0)

    def speed_one(c):
        mine = max1.at[gz]
        return remote(mine, mine, x1_s.at[c], x1_r.at[c], (gx, gy, (gz + c) % 8))

    def speed_two(e):
        to = (plane + e) % 16
        return remote(max2.at[plane], max2.at[plane], x2_s.at[e], x2_r.at[e], (to // 4, to % 4, gz))

    start_all(speed_one, 1, 8)
    store_rest = pltpu.make_async_copy(fields.at[pl.ds(5, 11)], out.at[pl.ds(5, 11)], out_sem.at[0])
    store_rest.start()

    rim_copies = []

    def rim_send(src, dst, device):
        k = len(rim_copies)
        copy = remote(src, dst, rim_s.at[k], rim_r.at[k], device)
        copy.start()
        rim_copies.append(copy)

    rim_send(fields.at[pl.ds(0, 4), pl.ds(112, 16)], xrecv.at[0], at(1, 0, 0))
    rim_send(fields.at[pl.ds(0, 4), pl.ds(0, 16)], xrecv.at[1], at(-1, 0, 0))
    for f in range(4):
        planes = fields[f].reshape(8, 16, 128)
        ysend[0, f] = planes[:, 0]
        ysend[1, f] = planes[:, 15]
    rim_send(ysend.at[1], yrecv.at[0], at(0, 1, 0))
    rim_send(ysend.at[0], yrecv.at[1], at(0, -1, 0))
    for dx in (1, -1):
        for dy in (1, -1):
            rim_send(ysend.at[(1 + dy) // 2], erecv.at[(1 - dx) // 2, (1 - dy) // 2], at(dx, dy, 0))

    def columns(x, carry):
        low, high = carry
        for f in range(4):
            l = (x + 1) * 4 + f
            rolled = pltpu.roll(fields[f, pl.ds(pl.multiple_of(x * 16, 16), 16), :], l, 1)
            low = jnp.where(lane16 == l, rolled, low)
            high = jnp.where(lane16 == l - 1, rolled, high)
        return low, high

    low, high = lax.fori_loop(0, 8, columns, (zeros, zeros))
    zcol[0] = low
    zcol[1] = pltpu.roll(high, 1, 1)
    for dx in (0, 1, -1):
        for dy in (0, 1, -1):
            rim_send(zcol.at[1], zcolr.at[0, 1 - dx, 1 - dy], at(dx, dy, 1))
            rim_send(zcol.at[0], zcolr.at[1, 1 - dx, 1 - dy], at(dx, dy, -1))

    recv_all(speed_one, 1, 8)
    max2[plane] = jnp.max(max1[...], axis=0)
    start_all(speed_two, 1, 16)

    for copy in rim_copies:
        copy.wait_recv()
    sub8 = lax.broadcasted_iota(jnp.int32, (8, 128), 0)
    no_xl, no_xh = gx == 0, gx == 3
    no_yl, no_yh = gy == 0, gy == 3

    def tail(above, below):
        above = jnp.where(no_yh, 0.0, above)
        below = jnp.where(no_yl, 0.0, below)
        return jnp.where(sub8 == 7, below, above)

    for f in range(4):
        for x in range(8):
            rim[f, x + 1, 0:16] = fields[f, x * 16 : x * 16 + 16]
            rim[f, x + 1, 16:24] = tail(
                jnp.broadcast_to(yrecv[1, f, x : x + 1], (8, 128)), jnp.broadcast_to(yrecv[0, f, x : x + 1], (8, 128))
            )
        for side, x, none, edge in ((0, 0, no_xl, 7), (1, 9, no_xh, 0)):
            rim[f, x, 0:16] = jnp.where(none, 0.0, xrecv[side, f])
            rim[f, x, 16:24] = jnp.where(
                none,
                0.0,
                tail(
                    jnp.broadcast_to(erecv[side, 1, f, edge : edge + 1], (8, 128)),
                    jnp.broadcast_to(erecv[side, 0, f, edge : edge + 1], (8, 128)),
                ),
            )

    lane24 = lax.broadcasted_iota(jnp.int32, (24, 128), 1)

    def gathered(side, none):
        tiles = []
        for dx in range(3):
            tiles.append(
                jnp.concatenate(
                    [zcolr[side, dx, 1], tail(zcolr[side, dx, 2, 0:8], zcolr[side, dx, 0, 8:16])], axis=0
                )
            )
        below = jnp.where(no_xl, 0.0, pltpu.roll(tiles[0], 96, 1))
        above = jnp.where(no_xh, 0.0, pltpu.roll(tiles[2], 32, 1))
        whole = jnp.where(lane24 < 4, below, jnp.where(lane24 < 36, tiles[1], above))
        return jnp.where(none, 0.0, whole)

    z_low = gathered(0, gz == 0)
    z_high = gathered(1, gz == 7)

    def along_z(f, x):
        q = rim[f, x]
        l = x * 4 + f
        before = jnp.where(lane24 == 0, pltpu.roll(z_low, (128 - l) % 128, 1), pltpu.roll(q, 1, 1))
        after = jnp.where(lane24 == 127, pltpu.roll(z_high, 127 - l, 1), pltpu.roll(q, 127, 1))
        return before + 2.0 * q + after, after - before

    def smooth_y(v):
        return (pltpu.roll(v, 1, 0) + 2.0 * v + pltpu.roll(v, 23, 0))[0:16]

    def spread_y(v):
        return (pltpu.roll(v, 23, 0) - pltpu.roll(v, 1, 0))[0:16]

    def plane_terms(x):
        p_s, p_d = along_z(0, x)
        u_s, _ = along_z(1, x)
        v_s, _ = along_z(2, x)
        _, w_d = along_z(3, x)
        return (
            smooth_y(p_s), spread_y(p_s), smooth_y(p_d),
            smooth_y(u_s), spread_y(v_s) + smooth_y(w_d),
        )

    def differences(x, carry):
        before, here = carry
        after = plane_terms(x + 1)
        gradient = (
            after[0] - before[0],
            before[1] + 2.0 * here[1] + after[1],
            before[2] + 2.0 * here[2] + after[2],
        )
        divergence = after[3] - before[3] + (before[4] + 2.0 * here[4] + after[4])
        rim[3, x - 1, 0:16] = divergence * (1.0 / 32.0)
        for k in range(3):
            rim[k, x - 1, 0:16] = gradient[k] * (1.0 / 32.0)
        return here, after

    lax.fori_loop(1, 9, differences, (plane_terms(0), plane_terms(1)))
    recv_all(speed_two, 1, 16)
    largest = jnp.max(jnp.max(max2[...], axis=0), axis=(0, 1), keepdims=True)
    step = 0.5 / jnp.sqrt(1.0 + 0.05 * largest)
    step = jnp.broadcast_to(step, (16, 128))

    def advance(x, carry):
        rows = pl.ds(pl.multiple_of(x * 16, 16), 16)
        divergence = rim[3, x, 0:16]
        pressure = fields[0, rows]
        fields[4, rows] = fields[4, rows] - step * pressure * divergence
        fields[0, rows] = pressure - step * divergence
        for k in range(3):
            fields[1 + k, rows] = fields[1 + k, rows] - step * rim[k, x, 0:16]
        return carry

    for copy in rim_copies:
        copy.wait_send()
    lax.fori_loop(0, 8, advance, 0)
    store = pltpu.make_async_copy(fields.at[pl.ds(0, 5)], out.at[pl.ds(0, 5)], out_sem.at[1])
    store.start()
    for copy in (z_up, z_down, x_up, x_down, y_up, y_down):
        copy.wait_send()
    sent_all(meta_one, 1, 8)
    sent_all(meta_two, 1, 16)
    sent_all(delivery, 0, 127)
    sent_all(speed_one, 1, 8)
    sent_all(speed_two, 1, 16)
    store_rest.wait()
    store.wait()


def on_device(old_state, remap_weights, new_owner, new_block):
    dma = pltpu.SemaphoreType.DMA
    any_space = pl.BlockSpec(memory_space=pl.ANY)
    vmem = pl.BlockSpec(memory_space=pltpu.VMEM)
    out = pl.pallas_call(
        kernel,
        out_shape=jax.ShapeDtypeStruct((16, 128, 128), F32),
        in_specs=[any_space, any_space, vmem, vmem],
        out_specs=any_space,
        scratch_shapes=[
            pltpu.VMEM((128, 512, 128), BF16),
            pltpu.VMEM((16, 8, 16, 128), F32),
            pltpu.VMEM((10, 18, 16, 128), F32),
            pltpu.VMEM((2, 16, 128), F32),
            pltpu.VMEM((2, 16, 128), F32),
            pltpu.VMEM((129, 16, 128), F32),
            pltpu.VMEM((128, 2, 16, 128), F32),
            pltpu.VMEM((128, 2, 16, 128), F32),
            pltpu.VMEM((16, 8, 2, 128), jnp.int32),
            pltpu.VMEM((2, 128, 128), jnp.int32),
            pltpu.VMEM((8, 128), jnp.int32),
            pltpu.SMEM((8, 128), jnp.int32),
            pltpu.VMEM((CHUNKS, 128, 128), BF16),
            pltpu.VMEM((16, 128, 128), BF16),
            pltpu.VMEM((16, 128, 128), F32),
            pltpu.VMEM((4, 10, 24, 128), F32),
            pltpu.VMEM((2, 4, 16, 128), F32),
            pltpu.VMEM((2, 4, 8, 128), F32),
            pltpu.VMEM((2, 4, 8, 128), F32),
            pltpu.VMEM((2, 2, 4, 8, 128), F32),
            pltpu.VMEM((2, 16, 128), F32),
            pltpu.VMEM((2, 3, 3, 16, 128), F32),
            pltpu.VMEM((8, 8, 128), F32),
            pltpu.VMEM((16, 8, 128), F32),
            dma((8,)), dma((1,)), dma((1,)), dma((2,)),
            dma((6,)), dma((6,)),
            dma((8,)), dma((8,)), dma((16,)), dma((16,)),
            dma((128,)), dma((128,)),
            dma((26,)), dma((26,)),
            dma((8,)), dma((8,)), dma((16,)), dma((16,)),
        ],
        compiler_params=pltpu.CompilerParams(
            collective_id=0, has_side_effects=True, vmem_limit_bytes=48 * 2**20
        ),
        cost_estimate=pl.CostEstimate(flops=2 * 16 * 512 * 128 * 128, bytes_accessed=20 * 2**20, transcendentals=0),
    )(
        old_state,
        remap_weights.reshape(128, 512, 128),
        new_owner.reshape(1, 128),
        new_block.reshape(1, 128),
    )
    return out.reshape(16, 8, 16, 128)


def solution(mesh):
    return jax.shard_map(
        on_device,
        mesh=mesh,
        in_specs=(
            P(None, "gx", "gy", "gz"),
            P(("gx", "gy", "gz"), None, None, None),
            P(("gx", "gy", "gz"), None),
            P(("gx", "gy", "gz")),
        ),
        out_specs=P(None, "gx", "gy", "gz"),
        check_vma=False,
    )
```

time: 226 us -> 66.8 us (0.30)
  Pallas kernels: 0 us -> 63.1 us
  blocking collectives: 62.3 us -> 0 us
  starting transfers between devices: 53 us -> 0 us
  waiting for transfers between devices: 39 us -> 0 us
  local copies, waits for them, and re-layouts: 40.2 us -> 3.51 us
  other arithmetic: 22.3 us -> 0 us
  matrix products: 7.02 us -> 0 us
    pallas_call x0 -> x1, Pallas kernels: none -> 63.1 us  [on_device(): pl.pallas_call(kernel, out_shape=jax.ShapeDtypeStruct((16, 128, 128), F32...]
    pmax x1 -> x0, blocking collectives: 62.3 us -> none  [on_device(): speed_max = lax.pmax(jnp.max(wave_speed(fields)), ('gx', 'gy', 'gz'))]
    ppermute x12 -> x0, starting transfers between devices: 30.5 us -> none  [the longest x6 21 us: padded_2(): before = lax.ppermute(last, axis, up)]
    all_to_all x2 -> x0, waiting for transfers between devices: 28.2 us -> none  [the longest x1 28.2 us: on_device(): lax.all_to_all(outgoing, ('gx', 'gy', 'gz'), split_axis=0, concat_axis=0,...]
    all_to_all x2 -> x0, starting transfers between devices: 22.5 us -> none  [the longest x1 12.6 us: on_device(): lax.all_to_all(target_ids, ('gx', 'gy', 'gz'), split_axis=0, concat_axis=...]
    scatter x2 -> x0, local copies, waits for them, and re-layouts: 14.8 us -> none  [the longest x1 13.7 us: on_device(): outgoing = jnp.zeros((slots_total, fields_count, cells_z), jnp.float32).a...]
    ppermute x12 -> x0, waiting for transfers between devices: 10.8 us -> none  [the longest x6 10.4 us: padded_2(): after = lax.ppermute(first, axis, down)]
    slice x10 -> x0, local copies, waits for them, and re-layouts: 10.7 us -> none  [the longest x5 6.82 us: padded_2(): last = lax.slice_in_dim(array, length - width, length, axis=dim)]
  transfers between devices with their start and end apart: 14 -> 0, of which waited for: 5 -> 0; matrix products, arithmetic and copies ran while one was open for 22% -> 0% of each run, Pallas kernels for 0% -> 0%
where the time goes in v1:
time: 66.8 us; the launch traced here: 66.6 us
  Pallas kernels  63.1 us (94%)
  local copies, waits for them, and re-layouts  3.51 us (5%)
    pallas_call x1, Pallas kernels, on_device(): pl.pallas_call(kernel, out_shape=jax.ShapeDtypeStruct((16, 128, 128), F32...  63.1 us
    unnamed x7, local copies, waits for them, and re-layouts  3.51 us

profile of v1, /device:TPU:1, one launch (start us, length us, event | category | flops | bytes accessed | tf_op | source)
XLA Modules:
  0.0 66.6 jit_solution(6307609214934157964)
XLA Ops:
  0.0 0.0 copy-start
  0.0 1.2 %copy-done = f32[16,8,16,128]{3,2,1,0:T(8,128)S(1)} copy-done((f32[16,8,16,128]{3,2,1,0:T(8,128)S(1)}, f32[16,8,16,128]{3,2,1,0:T(8,128)}, u32[]{:S(2)}) %copy-start) | copy-done | bytes 1048600
  1.2 0.0 copy-start.1
  1.2 0.7 copy-done.1
  1.9 0.0 copy-start.2
  1.9 0.7 copy-done.2
  2.5 63.1 %shard_map.46 = f32[16,128,128]{2,1,0:T(8,128)S(1)} custom-call(f32[16,8,16,128]{3,2,1,0:T(8,128)S(1)} %copy-done, bf16[128,512,128]{2,1,0:T(8,128)(2,1)} %bitcast.7, s32[1,128]{1,0:T(1,128)S(1)} %bitcast.5, s32[1,128]{1,0:T(1,128)S(1)} %bitcast.6), custom_call_target="tpu_custom_call" | custom-call | flops 268435456 | bytes 20971520 | tf_op jit(solution)/shard_map/pallas_call | solution.py:444
  65.7 1.0 %copy.6 = f32[16,8,16,128]{3,2,1,0:T(8,128)} copy(f32[16,8,16,128]{3,2,1,0:T(8,128)S(1)} %bitcast.4) | data formatting | bytes 2097152
Async XLA Ops:
  0.0 1.2 %copy-start = (f32[16,8,16,128]{3,2,1,0:T(8,128)S(1)}, f32[16,8,16,128]{3,2,1,0:T(8,128)}, u32[]{:S(2)}) copy-start(f32[16,8,16,128]{3,2,1,0:T(8,128)} %state.1) | copy-start | bytes 3145732
  1.2 0.7 copy-start.1
  1.9 0.7 copy-start.2

commit v2 on v1

--- a/solution.py
+++ b/solution.py
@@ -1,5 +1,6 @@
 import jax
 import jax.numpy as jnp
+import numpy as np
 from jax import lax
 from jax.experimental import pallas as pl
 from jax.experimental.pallas import tpu as pltpu
@@ -8,20 +9,22 @@
 MESH = pl.DeviceIdType.MESH
 F32 = jnp.float32
 BF16 = jnp.bfloat16
-CHUNKS = 4
-STEPS = 128 // CHUNKS
-
-
-def four(j):
-    return (2 + j * (j + 1) // 2) % 4
-
-
-def eight(j):
-    return (4 + ((j + 1) // 2) * (2 * (j % 2) - 1) + 8) % 8
-
-
-def offsets(i):
-    return four(i % 4), four((i // 4 + i + 1) % 4), eight((i // 16 + i // 4 + i + 2) % 8)
+CHUNKS = ((0, 32), (32, 64), (64, 96), (96, 128))
+
+
+def far_first():
+    draws = np.random.RandomState(0).permutation(128)
+    cells = [(int(t) // 32, int(t) // 8 % 4, int(t) % 8) for t in draws if t]
+    cells.sort(key=lambda o: -(min(o[0], 4 - o[0]) + min(o[1], 4 - o[1]) + min(o[2], 8 - o[2]) / 2))
+    order = []
+    for a, b, c in cells:
+        for offset in ((a, b, c), (-a % 4, -b % 4, -c % 8)):
+            if offset not in order:
+                order.append(offset)
+    return order + [(0, 0, 0)]
+
+
+OFFSETS = far_first()
 
 
 def limit(below, above):
@@ -29,10 +32,10 @@
 
 
 def kernel(
-    state, weights, owner, block, out,
-    w, nat, pad, zsend, zrecv, contrib, sendbuf, recvbuf, meta, metat, slotv, slots, lhs, rhs, fields, rim,
+    state, weights, owner_in, block_in, out,
+    w, nat, owner, block, pad, zsend, zrecv, contrib, sendbuf, recvbuf, meta, metat, slotv, slots, lhs, rhs, fields, rim,
     xrecv, ysend, yrecv, erecv, zcol, zcolr, max1, max2,
-    w_sem, in_sem, slot_sem, out_sem, halo_s, halo_r, m1_s, m1_r, m2_s, m2_r, a2a_s, a2a_r, rim_s, rim_r,
+    lines_sem, w_sem, in_sem, slot_sem, out_sem, halo_s, halo_r, m1_s, m1_r, m2_s, m2_r, a2a_s, a2a_r, rim_s, rim_r,
     x1_s, x1_r, x2_s, x2_r,
 ):
     gx, gy, gz = lax.axis_index("gx"), lax.axis_index("gy"), lax.axis_index("gz")
@@ -40,7 +43,7 @@
     me = plane * 8 + gz
 
     def at(a, b, c):
-        return ((gx + a + 4) % 4, (gy + b + 4) % 4, (gz + c + 8) % 8)
+        return (lax.rem(gx + a % 4, 4), lax.rem(gy + b % 4, 4), lax.rem(gz + c % 8, 8))
 
     def remote(src, dst, send, recv, device):
         return pltpu.make_async_remote_copy(
@@ -48,34 +51,30 @@
         )
 
     load_state = pltpu.make_async_copy(state, nat, in_sem.at[0])
-    load_state.start()
+    load_owner = pltpu.make_async_copy(owner_in, owner, in_sem.at[1])
+    load_block = pltpu.make_async_copy(block_in, block, in_sem.at[2])
+    for copy in (load_owner, load_block, load_state):
+        copy.start()
 
     def load_weights(x):
         return pltpu.make_async_copy(weights.at[pl.ds(x * 16, 16)], w.at[pl.ds(x * 16, 16)], w_sem.at[x])
 
-    for x in (1, 2, 3, 4, 5, 6, 0, 7):
-        load_weights(x).start()
     barrier = pltpu.get_barrier_semaphore()
 
-    def greet(t, carry):
-        pl.semaphore_signal(
-            barrier, inc=1, device_id=((gx + t // 32) % 4, (gy + (t // 8) % 4) % 4, (gz + t % 8) % 8),
-            device_id_type=MESH,
-        )
+
+    def greet_line(c, carry):
+        pl.semaphore_signal(barrier, inc=1, device_id=(gx, gy, lax.rem(gz + c, 8)), device_id_type=MESH)
         return carry
 
-    lax.fori_loop(1, 128, greet, 0)
-
-    lane = lax.broadcasted_iota(jnp.int32, (128, 128), 1)
-    sub = lax.broadcasted_iota(jnp.int32, (128, 128), 0)
-    named = jnp.broadcast_to(owner[...], (128, 128)).T == lane
-    first = jnp.min(jnp.where(named, sub, 128), axis=0, keepdims=True)
-    last = jnp.max(jnp.where(named, sub, -1), axis=0, keepdims=True)
-    slotv[...] = jnp.concatenate([first, jnp.where(last > first, last, 128)] * 4, axis=0)
-    fetch_slots = pltpu.make_async_copy(slotv, slots, slot_sem.at[0])
-    fetch_slots.start()
-    meta[plane, gz] = jnp.concatenate([owner[...], block[...]], axis=0)
-    contrib[128] = jnp.zeros((16, 128), F32)
+    def greet_plane(semaphore):
+        def body(e, carry):
+            to = lax.rem(plane + e, 16)
+            pl.semaphore_signal(semaphore, inc=1, device_id=(lax.div(to, 4), lax.rem(to, 4), gz), device_id_type=MESH)
+            return carry
+        lax.fori_loop(1, 16, body, 0)
+
+    greet_plane(barrier)
+    lax.fori_loop(1, 8, greet_line, 0)
 
     load_state.wait()
     lane16 = lax.broadcasted_iota(jnp.int32, (16, 128), 1)
@@ -97,7 +96,7 @@
     low, high = lax.fori_loop(0, 8, to_blocks, (zeros, zeros))
     zsend[0] = low
     zsend[1] = pltpu.roll(high, 1, 1)
-    pl.semaphore_wait(barrier, 127)
+    pl.semaphore_wait(barrier, 22)
 
     z_up = remote(zsend.at[1], zrecv.at[0], halo_s.at[0], halo_r.at[0], at(0, 0, 1))
     z_down = remote(zsend.at[0], zrecv.at[1], halo_s.at[1], halo_r.at[1], at(0, 0, -1))
@@ -112,11 +111,11 @@
 
     def meta_one(c):
         mine = meta.at[plane, gz]
-        return remote(mine, mine, m1_s.at[c], m1_r.at[c], (gx, gy, (gz + c) % 8))
+        return remote(mine, mine, m1_s.at[c], m1_r.at[c], (gx, gy, lax.rem(gz + c, 8)))
 
     def meta_two(e):
-        to = (plane + e) % 16
-        return remote(meta.at[plane], meta.at[plane], m2_s.at[e], m2_r.at[e], (to // 4, to % 4, gz))
+        to = lax.rem(plane + e, 16)
+        return remote(meta.at[plane], meta.at[plane], m2_s.at[e], m2_r.at[e], (lax.div(to, 4), lax.rem(to, 4), gz))
 
     def start_all(make, lo, hi):
         def body(i, carry):
@@ -136,6 +135,13 @@
             return carry
         lax.fori_loop(lo, hi, body, 0)
 
+    for x in (1, 2, 3, 4, 5, 6, 0, 7):
+        load_weights(x).start()
+
+    greet_plane(lines_sem)
+    load_owner.wait()
+    load_block.wait()
+    meta[plane, gz] = jnp.concatenate([owner[...], block[...]], axis=0)
     start_all(meta_one, 1, 8)
 
     z_up.wait_recv()
@@ -166,8 +172,15 @@
         return carry
 
     lax.fori_loop(2, 8, inner_plane, 0)
-    recv_all(meta_one, 1, 8)
-    start_all(meta_two, 1, 16)
+    lane = lax.broadcasted_iota(jnp.int32, (128, 128), 1)
+    sub = lax.broadcasted_iota(jnp.int32, (128, 128), 0)
+    named = jnp.broadcast_to(owner[...], (128, 128)).T == lane
+    first = jnp.min(jnp.where(named, sub, 128), axis=0, keepdims=True)
+    last = jnp.max(jnp.where(named, sub, -1), axis=0, keepdims=True)
+    slotv[...] = jnp.concatenate([first, jnp.where(last > first, last, 128)] * 4, axis=0)
+    fetch_slots = pltpu.make_async_copy(slotv, slots, slot_sem.at[0])
+    fetch_slots.start()
+    contrib[128] = jnp.zeros((16, 128), F32)
     for copy in (x_up, x_down, y_up, y_down):
         copy.wait_recv()
 
@@ -203,35 +216,36 @@
 
     lax.fori_loop(0, 2, side_planes, 0)
     fetch_slots.wait()
-
-    def delivery(i):
-        a, b, c = offsets(i)
-        return remote(sendbuf.at[i], recvbuf.at[i], a2a_s.at[i], a2a_r.at[i], at(a, b, c))
-
-    def deliver(i, carry):
-        a, b, c = offsets(i)
-        x, y, z = at(a, b, c)
-        to = x * 32 + y * 8 + z
+    pl.semaphore_wait(lines_sem, 15)
+
+    def delivery(i, device):
+        return remote(sendbuf.at[i], recvbuf.at[i], a2a_s.at[i], a2a_r.at[i], device)
+
+    def any_delivery(i):
+        return delivery(i, at(0, 0, 1))
+
+    for i, offset in enumerate(OFFSETS):
+        device = at(*offset)
+        to = device[0] * 32 + device[1] * 8 + device[2]
         for slot in range(2):
-            sendbuf[i, slot] = contrib[jnp.clip(slots[slot, to], 0, 128)]
-        delivery(i).start()
-        return carry
-
-    lax.fori_loop(0, 127, deliver, 0)
-    for slot in range(2):
-        recvbuf[127, slot] = contrib[jnp.clip(slots[slot, me], 0, 128)]
+            held = contrib[jnp.clip(slots[slot, to], 0, 128)]
+            if i == 127:
+                recvbuf[i, slot] = held
+            else:
+                sendbuf[i, slot] = held
+        if i < 127:
+            delivery(i, device).start()
+        if i == 15:
+            recv_all(meta_one, 1, 8)
+            start_all(meta_two, 1, 16)
 
     recv_all(meta_two, 1, 16)
 
-    def in_order(i, carry):
-        a, b, c = offsets(i)
+    for i, (a, b, c) in enumerate(OFFSETS):
         x, y, z = at(-a, -b, -c)
         row = meta[x * 4 + y, z]
-        metat[0, pl.ds(i, 1), :] = row[0:1]
-        metat[1, pl.ds(i, 1), :] = row[1:2]
-        return carry
-
-    lax.fori_loop(0, 128, in_order, 0)
+        metat[0, i : i + 1, :] = row[0:1]
+        metat[1, i : i + 1, :] = row[1:2]
     mine = metat[0] == me
     target = metat[1].astype(F32)
     lane = lane.astype(F32)
@@ -241,41 +255,38 @@
     target_1 = jnp.max(jnp.where(mine & (lane == last) & (last > first), target, -1.0), axis=1, keepdims=True)
     hot_0 = jnp.where(target_0 == lane, 1.0, 0.0)
     hot_1 = jnp.where(target_1 == lane, 1.0, 0.0)
-    for chunk in range(CHUNKS):
-        rows = slice(chunk * STEPS, (chunk + 1) * STEPS)
+    for chunk, (start, stop) in enumerate(CHUNKS):
+        rows = slice(start, stop)
         both = jnp.concatenate([hot_0[rows], hot_1[rows], hot_0[rows], hot_1[rows]], axis=0)
         lhs[chunk] = both.T.astype(BF16)
 
-    for chunk in range(CHUNKS):
-        recv_all(delivery, chunk * STEPS, min((chunk + 1) * STEPS, 127))
-        for part in range(STEPS // 16):
+    for chunk, (start, stop) in enumerate(CHUNKS):
+        steps = stop - start
+        recv_all(any_delivery, start, min(stop, 127))
+        for part in range(steps // 16):
             for slot in range(2):
                 for half in range(2):
-                    tile = recvbuf[pl.ds(chunk * STEPS + part * 16, 16), slot, pl.ds(half * 8, 8), :]
+                    tile = recvbuf[pl.ds(start + part * 16, 16), slot, pl.ds(half * 8, 8), :]
                     tile = jnp.swapaxes(tile, 0, 1)
                     upper = tile.astype(BF16)
                     lower = (tile - upper.astype(F32)).astype(BF16)
-                    row = slot * STEPS + part * 16
+                    row = slot * steps + part * 16
                     rhs[pl.ds(half * 8, 8), pl.ds(row, 16), :] = upper
-                    rhs[pl.ds(half * 8, 8), pl.ds(2 * STEPS + row, 16), :] = lower
-
-        def accumulate(f, carry):
+                    rhs[pl.ds(half * 8, 8), pl.ds(2 * steps + row, 16), :] = lower
+        for f in range(16):
             part_sum = jnp.dot(lhs[chunk], rhs[f], preferred_element_type=F32)
             fields[f] = part_sum if chunk == 0 else fields[f] + part_sum
-            return carry
-
-        lax.fori_loop(0, 16, accumulate, 0)
 
     square = fields[4] * fields[4] + (fields[1] * fields[1] + fields[2] * fields[2] + fields[3] * fields[3])
     max1[gz] = jnp.max(square.reshape(16, 8, 128), axis=0)
 
     def speed_one(c):
         mine = max1.at[gz]
-        return remote(mine, mine, x1_s.at[c], x1_r.at[c], (gx, gy, (gz + c) % 8))
+        return remote(mine, mine, x1_s.at[c], x1_r.at[c], (gx, gy, lax.rem(gz + c, 8)))
 
     def speed_two(e):
-        to = (plane + e) % 16
-        return remote(max2.at[plane], max2.at[plane], x2_s.at[e], x2_r.at[e], (to // 4, to % 4, gz))
+        to = lax.rem(plane + e, 16)
+        return remote(max2.at[plane], max2.at[plane], x2_s.at[e], x2_r.at[e], (lax.div(to, 4), lax.rem(to, 4), gz))
 
     start_all(speed_one, 1, 8)
     store_rest = pltpu.make_async_copy(fields.at[pl.ds(5, 11)], out.at[pl.ds(5, 11)], out_sem.at[0])
@@ -333,22 +344,17 @@
         below = jnp.where(no_yl, 0.0, below)
         return jnp.where(sub8 == 7, below, above)
 
-    for f in range(4):
-        for x in range(8):
-            rim[f, x + 1, 0:16] = fields[f, x * 16 : x * 16 + 16]
-            rim[f, x + 1, 16:24] = tail(
-                jnp.broadcast_to(yrecv[1, f, x : x + 1], (8, 128)), jnp.broadcast_to(yrecv[0, f, x : x + 1], (8, 128))
-            )
-        for side, x, none, edge in ((0, 0, no_xl, 7), (1, 9, no_xh, 0)):
-            rim[f, x, 0:16] = jnp.where(none, 0.0, xrecv[side, f])
-            rim[f, x, 16:24] = jnp.where(
-                none,
-                0.0,
-                tail(
-                    jnp.broadcast_to(erecv[side, 1, f, edge : edge + 1], (8, 128)),
-                    jnp.broadcast_to(erecv[side, 0, f, edge : edge + 1], (8, 128)),
-                ),
-            )
+    def row(ref, *index):
+        return jnp.broadcast_to(ref[index], (8, 128))
+
+    def padded(f, x):
+        if 1 <= x <= 8:
+            cells = fields[f, (x - 1) * 16 : x * 16]
+            edge = slice(x - 1, x)
+            return jnp.concatenate([cells, tail(row(yrecv, 1, f, edge), row(yrecv, 0, f, edge))], axis=0)
+        side, none, edge = (0, no_xl, slice(7, 8)) if x == 0 else (1, no_xh, slice(0, 1))
+        rows = tail(row(erecv, side, 1, f, edge), row(erecv, side, 0, f, edge))
+        return jnp.where(none, 0.0, jnp.concatenate([xrecv[side, f], rows], axis=0))
 
     lane24 = lax.broadcasted_iota(jnp.int32, (24, 128), 1)
 
@@ -369,7 +375,7 @@
     z_high = gathered(1, gz == 7)
 
     def along_z(f, x):
-        q = rim[f, x]
+        q = padded(f, x)
         l = x * 4 + f
         before = jnp.where(lane24 == 0, pltpu.roll(z_low, (128 - l) % 128, 1), pltpu.roll(q, 1, 1))
         after = jnp.where(lane24 == 127, pltpu.roll(z_high, 127 - l, 1), pltpu.roll(q, 127, 1))
@@ -391,46 +397,45 @@
             smooth_y(u_s), spread_y(v_s) + smooth_y(w_d),
         )
 
-    def differences(x, carry):
-        before, here = carry
-        after = plane_terms(x + 1)
+    terms = [plane_terms(0), plane_terms(1)]
+    for x in range(8):
+        terms.append(plane_terms(x + 2))
+        before, here, after = terms[x : x + 3]
         gradient = (
             after[0] - before[0],
             before[1] + 2.0 * here[1] + after[1],
             before[2] + 2.0 * here[2] + after[2],
         )
         divergence = after[3] - before[3] + (before[4] + 2.0 * here[4] + after[4])
-        rim[3, x - 1, 0:16] = divergence * (1.0 / 32.0)
+        rim[3, x] = divergence * (1.0 / 32.0)
         for k in range(3):
-            rim[k, x - 1, 0:16] = gradient[k] * (1.0 / 32.0)
-        return here, after
-
-    lax.fori_loop(1, 9, differences, (plane_terms(0), plane_terms(1)))
+            rim[k, x] = gradient[k] * (1.0 / 32.0)
+
+    for copy in rim_copies:
+        copy.wait_send()
     recv_all(speed_two, 1, 16)
     largest = jnp.max(jnp.max(max2[...], axis=0), axis=(0, 1), keepdims=True)
     step = 0.5 / jnp.sqrt(1.0 + 0.05 * largest)
     step = jnp.broadcast_to(step, (16, 128))
 
-    def advance(x, carry):
-        rows = pl.ds(pl.multiple_of(x * 16, 16), 16)
-        divergence = rim[3, x, 0:16]
+    def advance(x):
+        rows = slice(x * 16, x * 16 + 16)
+        divergence = rim[3, x]
         pressure = fields[0, rows]
         fields[4, rows] = fields[4, rows] - step * pressure * divergence
         fields[0, rows] = pressure - step * divergence
         for k in range(3):
-            fields[1 + k, rows] = fields[1 + k, rows] - step * rim[k, x, 0:16]
-        return carry
-
-    for copy in rim_copies:
-        copy.wait_send()
-    lax.fori_loop(0, 8, advance, 0)
+            fields[1 + k, rows] = fields[1 + k, rows] - step * rim[k, x]
+
+    for x in range(8):
+        advance(x)
     store = pltpu.make_async_copy(fields.at[pl.ds(0, 5)], out.at[pl.ds(0, 5)], out_sem.at[1])
     store.start()
     for copy in (z_up, z_down, x_up, x_down, y_up, y_down):
         copy.wait_send()
     sent_all(meta_one, 1, 8)
     sent_all(meta_two, 1, 16)
-    sent_all(delivery, 0, 127)
+    sent_all(any_delivery, 0, 127)
     sent_all(speed_one, 1, 8)
     sent_all(speed_two, 1, 16)
     store_rest.wait()
@@ -439,16 +444,17 @@
 
 def on_device(old_state, remap_weights, new_owner, new_block):
     dma = pltpu.SemaphoreType.DMA
-    any_space = pl.BlockSpec(memory_space=pl.ANY)
-    vmem = pl.BlockSpec(memory_space=pltpu.VMEM)
+    hbm = pl.BlockSpec(memory_space=pltpu.HBM)
     out = pl.pallas_call(
         kernel,
         out_shape=jax.ShapeDtypeStruct((16, 128, 128), F32),
-        in_specs=[any_space, any_space, vmem, vmem],
-        out_specs=any_space,
+        in_specs=[hbm, hbm, hbm, hbm],
+        out_specs=hbm,
         scratch_shapes=[
             pltpu.VMEM((128, 512, 128), BF16),
             pltpu.VMEM((16, 8, 16, 128), F32),
+            pltpu.VMEM((1, 128), jnp.int32),
+            pltpu.VMEM((1, 128), jnp.int32),
             pltpu.VMEM((10, 18, 16, 128), F32),
             pltpu.VMEM((2, 16, 128), F32),
             pltpu.VMEM((2, 16, 128), F32),
@@ -459,10 +465,10 @@
             pltpu.VMEM((2, 128, 128), jnp.int32),
             pltpu.VMEM((8, 128), jnp.int32),
             pltpu.SMEM((8, 128), jnp.int32),
-            pltpu.VMEM((CHUNKS, 128, 128), BF16),
+            pltpu.VMEM((len(CHUNKS), 128, 128), BF16),
             pltpu.VMEM((16, 128, 128), BF16),
             pltpu.VMEM((16, 128, 128), F32),
-            pltpu.VMEM((4, 10, 24, 128), F32),
+            pltpu.VMEM((4, 8, 16, 128), F32),
             pltpu.VMEM((2, 4, 16, 128), F32),
             pltpu.VMEM((2, 4, 8, 128), F32),
             pltpu.VMEM((2, 4, 8, 128), F32),
@@ -471,7 +477,8 @@
             pltpu.VMEM((2, 3, 3, 16, 128), F32),
             pltpu.VMEM((8, 8, 128), F32),
             pltpu.VMEM((16, 8, 128), F32),
-            dma((8,)), dma((1,)), dma((1,)), dma((2,)),
+            pltpu.SemaphoreType.REGULAR,
+            dma((8,)), dma((3,)), dma((1,)), dma((2,)),
             dma((6,)), dma((6,)),
             dma((8,)), dma((8,)), dma((16,)), dma((16,)),
             dma((128,)), dma((128,)),
@@ -479,7 +486,7 @@
             dma((8,)), dma((8,)), dma((16,)), dma((16,)),
         ],
         compiler_params=pltpu.CompilerParams(
-            collective_id=0, has_side_effects=True, vmem_limit_bytes=48 * 2**20
+            collective_id=0, has_side_effects=True, vmem_limit_bytes=60 * 2**20
         ),
         cost_estimate=pl.CostEstimate(flops=2 * 16 * 512 * 128 * 128, bytes_accessed=20 * 2**20, transcendentals=0),
     )(

time: 66.8 us -> 59.3 us (0.89)
  Pallas kernels: 63.1 us -> 56.9 us
  local copies, waits for them, and re-layouts: 3.51 us -> 2.29 us
    pallas_call x1, Pallas kernels: 63.1 us -> 56.9 us  [on_device(): pl.pallas_call(kernel, out_shape=jax.ShapeDtypeStruct((16, 128, 128), F32...]
    unnamed x7 -> x1, local copies, waits for them, and re-layouts: 3.51 us -> 2.29 us
where the time goes in v2:
time: 59.3 us; the launch traced here: 59.2 us
  Pallas kernels  56.9 us (96%)
  local copies, waits for them, and re-layouts  2.29 us (4%)
    pallas_call x1, Pallas kernels, on_device(): pl.pallas_call(kernel, out_shape=jax.ShapeDtypeStruct((16, 128, 128), F32...  56.9 us
    unnamed x1, local copies, waits for them, and re-layouts  2.29 us

profile of v2, /device:TPU:1, one launch (start us, length us, event | category | flops | bytes accessed | tf_op | source)
XLA Modules:
  0.0 59.2 jit_solution(7523806454823673566)
XLA Ops:
  0.0 56.9 %shard_map.46 = f32[16,128,128]{2,1,0:T(8,128)} custom-call(f32[16,8,16,128]{3,2,1,0:T(8,128)} %state.1, bf16[128,512,128]{2,1,0:T(8,128)(2,1)} %bitcast.4, s32[1,128]{1,0:T(1,128)} %bitcast.6, s32[1,128]{1,0:T(1,128)} %bitcast.7), custom_call_target="tpu_custom_call" | custom-call | flops 268435456 | bytes 20971520 | tf_op jit(solution)/shard_map/pallas_call | solution.py:448
  56.9 2.3 %copy.6 = f32[16,8,16,128]{3,2,1,0:T(8,128)} copy(f32[16,8,16,128]{3,2,1,0:T(8,128)} %bitcast.5) | data formatting | bytes 2097152

commit v3 on v2

--- a/solution.py
+++ b/solution.py
@@ -9,7 +9,9 @@
 MESH = pl.DeviceIdType.MESH
 F32 = jnp.float32
 BF16 = jnp.bfloat16
-CHUNKS = ((0, 32), (32, 64), (64, 96), (96, 128))
+CHUNKS = 4
+STEPS = 128 // CHUNKS
+HALO_Z, HALO, META_LINE, META_PLANE, RIM, SPEED_PLANE, SPEED_LINE, DELIVERY = range(8)
 
 
 def far_first():
@@ -35,20 +37,34 @@
     state, weights, owner_in, block_in, out,
     w, nat, owner, block, pad, zsend, zrecv, contrib, sendbuf, recvbuf, meta, metat, slotv, slots, lhs, rhs, fields, rim,
     xrecv, ysend, yrecv, erecv, zcol, zcolr, max1, max2,
-    lines_sem, w_sem, in_sem, slot_sem, out_sem, halo_s, halo_r, m1_s, m1_r, m2_s, m2_r, a2a_s, a2a_r, rim_s, rim_r,
-    x1_s, x1_r, x2_s, x2_r,
+    lines_sem, w_sem, in_sem, slot_sem, out_sem, sent, got,
 ):
     gx, gy, gz = lax.axis_index("gx"), lax.axis_index("gy"), lax.axis_index("gz")
-    plane = gx * 4 + gy
-    me = plane * 8 + gz
+    me = (gx * 4 + gy) * 8 + gz
+
+    def around(here, size):
+        steps = [here]
+        for step in range(1, size):
+            there = here + step
+            steps.append(jnp.where(there >= size, there - size, there))
+        return steps
+
+    xs, ys, zs = around(gx, 4), around(gy, 4), around(gz, 8)
 
     def at(a, b, c):
-        return (lax.rem(gx + a % 4, 4), lax.rem(gy + b % 4, 4), lax.rem(gz + c % 8, 8))
-
-    def remote(src, dst, send, recv, device):
+        return xs[a % 4], ys[b % 4], zs[c % 8]
+
+    def remote(src, dst, group, device, part=0):
         return pltpu.make_async_remote_copy(
-            src_ref=src, dst_ref=dst, send_sem=send, recv_sem=recv, device_id=device, device_id_type=MESH
+            src_ref=src, dst_ref=dst, send_sem=sent.at[group], recv_sem=got.at[group + part], device_id=device,
+            device_id_type=MESH,
         )
+
+    def received(ref, group, part=0):
+        remote(ref, ref, group, at(0, 0, 1), part).wait_recv()
+
+    def delivered(ref, group):
+        remote(ref, ref, group, at(0, 0, 1)).wait_send()
 
     load_state = pltpu.make_async_copy(state, nat, in_sem.at[0])
     load_owner = pltpu.make_async_copy(owner_in, owner, in_sem.at[1])
@@ -62,19 +78,14 @@
     barrier = pltpu.get_barrier_semaphore()
 
 
-    def greet_line(c, carry):
-        pl.semaphore_signal(barrier, inc=1, device_id=(gx, gy, lax.rem(gz + c, 8)), device_id_type=MESH)
-        return carry
-
-    def greet_plane(semaphore):
-        def body(e, carry):
-            to = lax.rem(plane + e, 16)
-            pl.semaphore_signal(semaphore, inc=1, device_id=(lax.div(to, 4), lax.rem(to, 4), gz), device_id_type=MESH)
-            return carry
-        lax.fori_loop(1, 16, body, 0)
-
-    greet_plane(barrier)
-    lax.fori_loop(1, 8, greet_line, 0)
+    def greet(semaphore, device):
+        pl.semaphore_signal(semaphore, inc=1, device_id=device, device_id_type=MESH)
+
+    plane = [(a, b) for a in range(4) for b in range(4)]
+    for a, b in plane[1:]:
+        greet(barrier, at(a, b, 0))
+    for c in range(1, 8):
+        greet(barrier, at(0, 0, c))
 
     load_state.wait()
     lane16 = lax.broadcasted_iota(jnp.int32, (16, 128), 1)
@@ -98,54 +109,26 @@
     zsend[1] = pltpu.roll(high, 1, 1)
     pl.semaphore_wait(barrier, 22)
 
-    z_up = remote(zsend.at[1], zrecv.at[0], halo_s.at[0], halo_r.at[0], at(0, 0, 1))
-    z_down = remote(zsend.at[0], zrecv.at[1], halo_s.at[1], halo_r.at[1], at(0, 0, -1))
     inner = pl.ds(1, 16)
     cells = pl.ds(1, 8)
-    x_up = remote(pad.at[8, inner], pad.at[0, inner], halo_s.at[2], halo_r.at[2], at(1, 0, 0))
-    x_down = remote(pad.at[1, inner], pad.at[9, inner], halo_s.at[3], halo_r.at[3], at(-1, 0, 0))
-    y_up = remote(pad.at[cells, 16], pad.at[cells, 0], halo_s.at[4], halo_r.at[4], at(0, 1, 0))
-    y_down = remote(pad.at[cells, 1], pad.at[cells, 17], halo_s.at[5], halo_r.at[5], at(0, -1, 0))
-    for copy in (z_up, z_down, x_up, x_down, y_up, y_down):
-        copy.start()
-
-    def meta_one(c):
-        mine = meta.at[plane, gz]
-        return remote(mine, mine, m1_s.at[c], m1_r.at[c], (gx, gy, lax.rem(gz + c, 8)))
-
-    def meta_two(e):
-        to = lax.rem(plane + e, 16)
-        return remote(meta.at[plane], meta.at[plane], m2_s.at[e], m2_r.at[e], (lax.div(to, 4), lax.rem(to, 4), gz))
-
-    def start_all(make, lo, hi):
-        def body(i, carry):
-            make(i).start()
-            return carry
-        lax.fori_loop(lo, hi, body, 0)
-
-    def recv_all(make, lo, hi):
-        def body(i, carry):
-            make(i).wait_recv()
-            return carry
-        lax.fori_loop(lo, hi, body, 0)
-
-    def sent_all(make, lo, hi):
-        def body(i, carry):
-            make(i).wait_send()
-            return carry
-        lax.fori_loop(lo, hi, body, 0)
-
+    remote(zsend.at[1], zrecv.at[0], HALO_Z, at(0, 0, 1)).start()
+    remote(zsend.at[0], zrecv.at[1], HALO_Z, at(0, 0, -1)).start()
+    remote(pad.at[8, inner], pad.at[0, inner], HALO, at(1, 0, 0)).start()
+    remote(pad.at[1, inner], pad.at[9, inner], HALO, at(-1, 0, 0)).start()
+    remote(pad.at[cells, 16], pad.at[cells, 0], HALO, at(0, 1, 0)).start()
+    remote(pad.at[cells, 1], pad.at[cells, 17], HALO, at(0, -1, 0)).start()
     for x in (1, 2, 3, 4, 5, 6, 0, 7):
         load_weights(x).start()
 
-    greet_plane(lines_sem)
+    for a, b in plane[1:]:
+        greet(lines_sem, at(a, b, 0))
     load_owner.wait()
     load_block.wait()
-    meta[plane, gz] = jnp.concatenate([owner[...], block[...]], axis=0)
-    start_all(meta_one, 1, 8)
-
-    z_up.wait_recv()
-    z_down.wait_recv()
+    meta[0, 0] = jnp.concatenate([owner[...], block[...]], axis=0)
+    for c in range(1, 8):
+        remote(meta.at[0, 0], meta.at[0, c], META_LINE, at(0, 0, c)).start()
+
+    received(zrecv, HALO_Z)
     z_low = jnp.where(gz == 0, 0.0, zrecv[0])
     z_high = jnp.where(gz == 7, 0.0, zrecv[1])
 
@@ -181,8 +164,7 @@
     fetch_slots = pltpu.make_async_copy(slotv, slots, slot_sem.at[0])
     fetch_slots.start()
     contrib[128] = jnp.zeros((16, 128), F32)
-    for copy in (x_up, x_down, y_up, y_down):
-        copy.wait_recv()
+    received(pad.at[0:3, inner], HALO)
 
     @pl.when(gx == 0)
     def _():
@@ -217,12 +199,6 @@
     lax.fori_loop(0, 2, side_planes, 0)
     fetch_slots.wait()
     pl.semaphore_wait(lines_sem, 15)
-
-    def delivery(i, device):
-        return remote(sendbuf.at[i], recvbuf.at[i], a2a_s.at[i], a2a_r.at[i], device)
-
-    def any_delivery(i):
-        return delivery(i, at(0, 0, 1))
 
     for i, offset in enumerate(OFFSETS):
         device = at(*offset)
@@ -234,16 +210,15 @@
             else:
                 sendbuf[i, slot] = held
         if i < 127:
-            delivery(i, device).start()
+            remote(sendbuf.at[i], recvbuf.at[i], DELIVERY, device, i // STEPS).start()
         if i == 15:
-            recv_all(meta_one, 1, 8)
-            start_all(meta_two, 1, 16)
-
-    recv_all(meta_two, 1, 16)
-
+            received(meta.at[0, 1:8], META_LINE)
+            for k, (a, b) in enumerate(plane[1:]):
+                remote(meta.at[0], meta.at[k + 1], META_PLANE, at(a, b, 0)).start()
+
+    received(meta.at[1:16], META_PLANE)
     for i, (a, b, c) in enumerate(OFFSETS):
-        x, y, z = at(-a, -b, -c)
-        row = meta[x * 4 + y, z]
+        row = meta[a * 4 + b, c]
         metat[0, i : i + 1, :] = row[0:1]
         metat[1, i : i + 1, :] = row[1:2]
     mine = metat[0] == me
@@ -255,50 +230,37 @@
     target_1 = jnp.max(jnp.where(mine & (lane == last) & (last > first), target, -1.0), axis=1, keepdims=True)
     hot_0 = jnp.where(target_0 == lane, 1.0, 0.0)
     hot_1 = jnp.where(target_1 == lane, 1.0, 0.0)
-    for chunk, (start, stop) in enumerate(CHUNKS):
-        rows = slice(start, stop)
+    for chunk in range(CHUNKS):
+        rows = slice(chunk * STEPS, (chunk + 1) * STEPS)
         both = jnp.concatenate([hot_0[rows], hot_1[rows], hot_0[rows], hot_1[rows]], axis=0)
         lhs[chunk] = both.T.astype(BF16)
 
-    for chunk, (start, stop) in enumerate(CHUNKS):
-        steps = stop - start
-        recv_all(any_delivery, start, min(stop, 127))
-        for part in range(steps // 16):
+    for chunk in range(CHUNKS):
+        start = chunk * STEPS
+        received(recvbuf.at[start : min(start + STEPS, 127)], DELIVERY, chunk)
+        for part in range(STEPS // 16):
             for slot in range(2):
                 for half in range(2):
                     tile = recvbuf[pl.ds(start + part * 16, 16), slot, pl.ds(half * 8, 8), :]
                     tile = jnp.swapaxes(tile, 0, 1)
                     upper = tile.astype(BF16)
                     lower = (tile - upper.astype(F32)).astype(BF16)
-                    row = slot * steps + part * 16
+                    row = slot * STEPS + part * 16
                     rhs[pl.ds(half * 8, 8), pl.ds(row, 16), :] = upper
-                    rhs[pl.ds(half * 8, 8), pl.ds(2 * steps + row, 16), :] = lower
+                    rhs[pl.ds(half * 8, 8), pl.ds(2 * STEPS + row, 16), :] = lower
         for f in range(16):
             part_sum = jnp.dot(lhs[chunk], rhs[f], preferred_element_type=F32)
             fields[f] = part_sum if chunk == 0 else fields[f] + part_sum
 
     square = fields[4] * fields[4] + (fields[1] * fields[1] + fields[2] * fields[2] + fields[3] * fields[3])
-    max1[gz] = jnp.max(square.reshape(16, 8, 128), axis=0)
-
-    def speed_one(c):
-        mine = max1.at[gz]
-        return remote(mine, mine, x1_s.at[c], x1_r.at[c], (gx, gy, lax.rem(gz + c, 8)))
-
-    def speed_two(e):
-        to = lax.rem(plane + e, 16)
-        return remote(max2.at[plane], max2.at[plane], x2_s.at[e], x2_r.at[e], (lax.div(to, 4), lax.rem(to, 4), gz))
-
-    start_all(speed_one, 1, 8)
+    max1[0] = jnp.max(square.reshape(16, 8, 128), axis=0)
+    for k, (a, b) in enumerate(plane[1:]):
+        remote(max1.at[0], max1.at[k + 1], SPEED_PLANE, at(a, b, 0)).start()
     store_rest = pltpu.make_async_copy(fields.at[pl.ds(5, 11)], out.at[pl.ds(5, 11)], out_sem.at[0])
     store_rest.start()
 
-    rim_copies = []
-
     def rim_send(src, dst, device):
-        k = len(rim_copies)
-        copy = remote(src, dst, rim_s.at[k], rim_r.at[k], device)
-        copy.start()
-        rim_copies.append(copy)
+        remote(src, dst, RIM, device).start()
 
     rim_send(fields.at[pl.ds(0, 4), pl.ds(112, 16)], xrecv.at[0], at(1, 0, 0))
     rim_send(fields.at[pl.ds(0, 4), pl.ds(0, 16)], xrecv.at[1], at(-1, 0, 0))
@@ -329,12 +291,12 @@
             rim_send(zcol.at[1], zcolr.at[0, 1 - dx, 1 - dy], at(dx, dy, 1))
             rim_send(zcol.at[0], zcolr.at[1, 1 - dx, 1 - dy], at(dx, dy, -1))
 
-    recv_all(speed_one, 1, 8)
-    max2[plane] = jnp.max(max1[...], axis=0)
-    start_all(speed_two, 1, 16)
-
-    for copy in rim_copies:
-        copy.wait_recv()
+    received(max1.at[1:16], SPEED_PLANE)
+    max2[0] = jnp.max(max1[...], axis=0)
+    for c in range(1, 8):
+        remote(max2.at[0], max2.at[c], SPEED_LINE, at(0, 0, c)).start()
+
+    received(contrib.at[0:38], RIM)
     sub8 = lax.broadcasted_iota(jnp.int32, (8, 128), 0)
     no_xl, no_xh = gx == 0, gx == 3
     no_yl, no_yh = gy == 0, gy == 3
@@ -411,9 +373,8 @@
         for k in range(3):
             rim[k, x] = gradient[k] * (1.0 / 32.0)
 
-    for copy in rim_copies:
-        copy.wait_send()
-    recv_all(speed_two, 1, 16)
+    delivered(contrib.at[0:38], RIM)
+    received(max2.at[1:8], SPEED_LINE)
     largest = jnp.max(jnp.max(max2[...], axis=0), axis=(0, 1), keepdims=True)
     step = 0.5 / jnp.sqrt(1.0 + 0.05 * largest)
     step = jnp.broadcast_to(step, (16, 128))
@@ -431,13 +392,13 @@
         advance(x)
     store = pltpu.make_async_copy(fields.at[pl.ds(0, 5)], out.at[pl.ds(0, 5)], out_sem.at[1])
     store.start()
-    for copy in (z_up, z_down, x_up, x_down, y_up, y_down):
-        copy.wait_send()
-    sent_all(meta_one, 1, 8)
-    sent_all(meta_two, 1, 16)
-    sent_all(any_delivery, 0, 127)
-    sent_all(speed_one, 1, 8)
-    sent_all(speed_two, 1, 16)
+    delivered(zsend, HALO_Z)
+    delivered(pad.at[0:3, inner], HALO)
+    delivered(meta.at[0, 1:8], META_LINE)
+    delivered(meta.at[1:16], META_PLANE)
+    delivered(sendbuf.at[0:127], DELIVERY)
+    delivered(max1.at[1:16], SPEED_PLANE)
+    delivered(max2.at[1:8], SPEED_LINE)
     store_rest.wait()
     store.wait()
 
@@ -465,7 +426,7 @@
             pltpu.VMEM((2, 128, 128), jnp.int32),
             pltpu.VMEM((8, 128), jnp.int32),
             pltpu.SMEM((8, 128), jnp.int32),
-            pltpu.VMEM((len(CHUNKS), 128, 128), BF16),
+            pltpu.VMEM((CHUNKS, 128, 128), BF16),
             pltpu.VMEM((16, 128, 128), BF16),
             pltpu.VMEM((16, 128, 128), F32),
             pltpu.VMEM((4, 8, 16, 128), F32),
@@ -475,15 +436,10 @@
             pltpu.VMEM((2, 2, 4, 8, 128), F32),
             pltpu.VMEM((2, 16, 128), F32),
             pltpu.VMEM((2, 3, 3, 16, 128), F32),
+            pltpu.VMEM((16, 8, 128), F32),
             pltpu.VMEM((8, 8, 128), F32),
-            pltpu.VMEM((16, 8, 128), F32),
             pltpu.SemaphoreType.REGULAR,
-            dma((8,)), dma((3,)), dma((1,)), dma((2,)),
-            dma((6,)), dma((6,)),
-            dma((8,)), dma((8,)), dma((16,)), dma((16,)),
-            dma((128,)), dma((128,)),
-            dma((26,)), dma((26,)),
-            dma((8,)), dma((8,)), dma((16,)), dma((16,)),
+            dma((8,)), dma((3,)), dma((1,)), dma((2,)), dma((8,)), dma((7 + CHUNKS,)),
         ],
         compiler_params=pltpu.CompilerParams(
             collective_id=0, has_side_effects=True, vmem_limit_bytes=60 * 2**20

time: 59.3 us -> 55.8 us (0.941)
  Pallas kernels: 56.9 us -> 53.3 us
    pallas_call x1, Pallas kernels: 56.9 us -> 53.3 us  [on_device(): pl.pallas_call(kernel, out_shape=jax.ShapeDtypeStruct((16, 128, 128), F32...]
where the time goes in v3:
time: 55.8 us; the launch traced here: 55.6 us
  Pallas kernels  53.3 us (96%)
  local copies, waits for them, and re-layouts  2.29 us (4%)
    pallas_call x1, Pallas kernels, on_device(): pl.pallas_call(kernel, out_shape=jax.ShapeDtypeStruct((16, 128, 128), F32...  53.3 us
    unnamed x1, local copies, waits for them, and re-layouts  2.29 us

profile of v3, /device:TPU:1, one launch (start us, length us, event | category | flops | bytes accessed | tf_op | source)
XLA Modules:
  0.0 55.6 jit_solution(8053068339954003283)
XLA Ops:
  0.0 53.3 %shard_map.46 = f32[16,128,128]{2,1,0:T(8,128)} custom-call(f32[16,8,16,128]{3,2,1,0:T(8,128)} %state.1, bf16[128,512,128]{2,1,0:T(8,128)(2,1)} %bitcast.4, s32[1,128]{1,0:T(1,128)} %bitcast.6, s32[1,128]{1,0:T(1,128)} %bitcast.7), custom_call_target="tpu_custom_call" | custom-call | flops 268435456 | bytes 20971520 | tf_op jit(solution)/shard_map/pallas_call | solution.py:409
  53.3 2.3 %copy.6 = f32[16,8,16,128]{3,2,1,0:T(8,128)} copy(f32[16,8,16,128]{3,2,1,0:T(8,128)} %bitcast.5) | data formatting | bytes 2097152

commit v4 on v3

--- a/solution.py
+++ b/solution.py
@@ -11,7 +11,7 @@
 BF16 = jnp.bfloat16
 CHUNKS = 4
 STEPS = 128 // CHUNKS
-HALO_Z, HALO, META_LINE, META_PLANE, RIM, SPEED_PLANE, SPEED_LINE, DELIVERY = range(8)
+HALO_Z, HALO, META_LINE, META_PLANE, RIM, SPEED_CORE, SPEED_CHIPS, DELIVERY = range(8)
 
 
 def far_first():
@@ -34,10 +34,10 @@
 
 
 def kernel(
-    state, weights, owner_in, block_in, out,
-    w, nat, owner, block, pad, zsend, zrecv, contrib, sendbuf, recvbuf, meta, metat, slotv, slots, lhs, rhs, fields, rim,
+    state, weights, numbers, fields,
+    w, nat, pad, zsend, zrecv, contrib, sendbuf, recvbuf, meta, metat, slotv, slots, lhs, rhs, rim,
     xrecv, ysend, yrecv, erecv, zcol, zcolr, max1, max2,
-    lines_sem, w_sem, in_sem, slot_sem, out_sem, sent, got,
+    lines_sem, w_sem, in_sem, slot_sem, sent, got,
 ):
     gx, gy, gz = lax.axis_index("gx"), lax.axis_index("gy"), lax.axis_index("gz")
     me = (gx * 4 + gy) * 8 + gz
@@ -67,10 +67,7 @@
         remote(ref, ref, group, at(0, 0, 1)).wait_send()
 
     load_state = pltpu.make_async_copy(state, nat, in_sem.at[0])
-    load_owner = pltpu.make_async_copy(owner_in, owner, in_sem.at[1])
-    load_block = pltpu.make_async_copy(block_in, block, in_sem.at[2])
-    for copy in (load_owner, load_block, load_state):
-        copy.start()
+    load_state.start()
 
     def load_weights(x):
         return pltpu.make_async_copy(weights.at[pl.ds(x * 16, 16)], w.at[pl.ds(x * 16, 16)], w_sem.at[x])
@@ -122,9 +119,7 @@
 
     for a, b in plane[1:]:
         greet(lines_sem, at(a, b, 0))
-    load_owner.wait()
-    load_block.wait()
-    meta[0, 0] = jnp.concatenate([owner[...], block[...]], axis=0)
+    meta[0, 0] = numbers[...]
     for c in range(1, 8):
         remote(meta.at[0, 0], meta.at[0, c], META_LINE, at(0, 0, c)).start()
 
@@ -157,7 +152,7 @@
     lax.fori_loop(2, 8, inner_plane, 0)
     lane = lax.broadcasted_iota(jnp.int32, (128, 128), 1)
     sub = lax.broadcasted_iota(jnp.int32, (128, 128), 0)
-    named = jnp.broadcast_to(owner[...], (128, 128)).T == lane
+    named = jnp.broadcast_to(numbers[0:1], (128, 128)).T == lane
     first = jnp.min(jnp.where(named, sub, 128), axis=0, keepdims=True)
     last = jnp.max(jnp.where(named, sub, -1), axis=0, keepdims=True)
     slotv[...] = jnp.concatenate([first, jnp.where(last > first, last, 128)] * 4, axis=0)
@@ -253,11 +248,10 @@
             fields[f] = part_sum if chunk == 0 else fields[f] + part_sum
 
     square = fields[4] * fields[4] + (fields[1] * fields[1] + fields[2] * fields[2] + fields[3] * fields[3])
+    own_core = lax.rem(gz, 2)
+    other_core = (gx, gy, gz + 1 - 2 * own_core)
     max1[0] = jnp.max(square.reshape(16, 8, 128), axis=0)
-    for k, (a, b) in enumerate(plane[1:]):
-        remote(max1.at[0], max1.at[k + 1], SPEED_PLANE, at(a, b, 0)).start()
-    store_rest = pltpu.make_async_copy(fields.at[pl.ds(5, 11)], out.at[pl.ds(5, 11)], out_sem.at[0])
-    store_rest.start()
+    remote(max1.at[0], max1.at[1], SPEED_CORE, other_core).start()
 
     def rim_send(src, dst, device):
         remote(src, dst, RIM, device).start()
@@ -291,10 +285,11 @@
             rim_send(zcol.at[1], zcolr.at[0, 1 - dx, 1 - dy], at(dx, dy, 1))
             rim_send(zcol.at[0], zcolr.at[1, 1 - dx, 1 - dy], at(dx, dy, -1))
 
-    received(max1.at[1:16], SPEED_PLANE)
-    max2[0] = jnp.max(max1[...], axis=0)
-    for c in range(1, 8):
-        remote(max2.at[0], max2.at[c], SPEED_LINE, at(0, 0, c)).start()
+    received(max1.at[1:2], SPEED_CORE)
+    max2[0] = jnp.max(jnp.maximum(max1[0], max1[1]), axis=0, keepdims=True)
+    chips = [offset for offset in OFFSETS if offset[2] % 2 == 0]
+    for k, offset in enumerate(chips[:63]):
+        remote(max2.at[0], max2.at[k + 1], SPEED_CHIPS, at(*offset)).start()
 
     received(contrib.at[0:38], RIM)
     sub8 = lax.broadcasted_iota(jnp.int32, (8, 128), 0)
@@ -374,8 +369,8 @@
             rim[k, x] = gradient[k] * (1.0 / 32.0)
 
     delivered(contrib.at[0:38], RIM)
-    received(max2.at[1:8], SPEED_LINE)
-    largest = jnp.max(jnp.max(max2[...], axis=0), axis=(0, 1), keepdims=True)
+    received(max2.at[1:64], SPEED_CHIPS)
+    largest = jnp.max(jnp.max(max2[...], axis=0), axis=1, keepdims=True)
     step = 0.5 / jnp.sqrt(1.0 + 0.05 * largest)
     step = jnp.broadcast_to(step, (16, 128))
 
@@ -390,32 +385,27 @@
 
     for x in range(8):
         advance(x)
-    store = pltpu.make_async_copy(fields.at[pl.ds(0, 5)], out.at[pl.ds(0, 5)], out_sem.at[1])
-    store.start()
     delivered(zsend, HALO_Z)
     delivered(pad.at[0:3, inner], HALO)
     delivered(meta.at[0, 1:8], META_LINE)
     delivered(meta.at[1:16], META_PLANE)
     delivered(sendbuf.at[0:127], DELIVERY)
-    delivered(max1.at[1:16], SPEED_PLANE)
-    delivered(max2.at[1:8], SPEED_LINE)
-    store_rest.wait()
-    store.wait()
+    delivered(max1.at[1:2], SPEED_CORE)
+    delivered(max2.at[1:64], SPEED_CHIPS)
 
 
 def on_device(old_state, remap_weights, new_owner, new_block):
     dma = pltpu.SemaphoreType.DMA
     hbm = pl.BlockSpec(memory_space=pltpu.HBM)
+    vmem = pl.BlockSpec(memory_space=pltpu.VMEM)
     out = pl.pallas_call(
         kernel,
         out_shape=jax.ShapeDtypeStruct((16, 128, 128), F32),
-        in_specs=[hbm, hbm, hbm, hbm],
-        out_specs=hbm,
+        in_specs=[hbm, hbm, vmem],
+        out_specs=vmem,
         scratch_shapes=[
             pltpu.VMEM((128, 512, 128), BF16),
             pltpu.VMEM((16, 8, 16, 128), F32),
-            pltpu.VMEM((1, 128), jnp.int32),
-            pltpu.VMEM((1, 128), jnp.int32),
             pltpu.VMEM((10, 18, 16, 128), F32),
             pltpu.VMEM((2, 16, 128), F32),
             pltpu.VMEM((2, 16, 128), F32),
@@ -428,7 +418,6 @@
             pltpu.SMEM((8, 128), jnp.int32),
             pltpu.VMEM((CHUNKS, 128, 128), BF16),
             pltpu.VMEM((16, 128, 128), BF16),
-            pltpu.VMEM((16, 128, 128), F32),
             pltpu.VMEM((4, 8, 16, 128), F32),
             pltpu.VMEM((2, 4, 16, 128), F32),
             pltpu.VMEM((2, 4, 8, 128), F32),
@@ -436,20 +425,19 @@
             pltpu.VMEM((2, 2, 4, 8, 128), F32),
             pltpu.VMEM((2, 16, 128), F32),
             pltpu.VMEM((2, 3, 3, 16, 128), F32),
-            pltpu.VMEM((16, 8, 128), F32),
-            pltpu.VMEM((8, 8, 128), F32),
+            pltpu.VMEM((2, 8, 128), F32),
+            pltpu.VMEM((64, 1, 128), F32),
             pltpu.SemaphoreType.REGULAR,
-            dma((8,)), dma((3,)), dma((1,)), dma((2,)), dma((8,)), dma((7 + CHUNKS,)),
+            dma((8,)), dma((1,)), dma((1,)), dma((8,)), dma((7 + CHUNKS,)),
         ],
         compiler_params=pltpu.CompilerParams(
-            collective_id=0, has_side_effects=True, vmem_limit_bytes=60 * 2**20
+            collective_id=0, has_side_effects=True, vmem_limit_bytes=52 * 2**20
         ),
         cost_estimate=pl.CostEstimate(flops=2 * 16 * 512 * 128 * 128, bytes_accessed=20 * 2**20, transcendentals=0),
     )(
         old_state,
         remap_weights.reshape(128, 512, 128),
-        new_owner.reshape(1, 128),
-        new_block.reshape(1, 128),
+        jnp.concatenate([new_owner.reshape(1, 128), new_block.reshape(1, 128)], axis=0),
     )
     return out.reshape(16, 8, 16, 128)
 

time: 55.8 us -> 52.3 us (0.937)
  Pallas kernels: 53.3 us -> 50.5 us
  local copies, waits for them, and re-layouts: 2.29 us -> 0.97 us
  other arithmetic: 0 us -> 0.68 us
    pallas_call x1, Pallas kernels: 53.3 us -> 50.5 us  [on_device(): pl.pallas_call(kernel, out_shape=jax.ShapeDtypeStruct((16, 128, 128), F32...]
    unnamed x1, local copies, waits for them, and re-layouts: 2.29 us -> 0.97 us
    concatenate x0 -> x1, other arithmetic: none -> 0.68 us  [on_device(): jnp.concatenate([new_owner.reshape(1, 128), new_block.reshape(1, 128)], a...]
where the time goes in v4:
time: 52.3 us; the launch traced here: 52.1 us
  Pallas kernels  50.5 us (97%)
  local copies, waits for them, and re-layouts  0.97 us (2%)
  other arithmetic  0.68 us (1%)
    pallas_call x1, Pallas kernels, on_device(): pl.pallas_call(kernel, out_shape=jax.ShapeDtypeStruct((16, 128, 128), F32...  50.5 us

profile of v4, /device:TPU:1, one launch (start us, length us, event | category | flops | bytes accessed | tf_op | source)
XLA Modules:
  0.0 52.1 jit_solution(11050592461710350902)
XLA Ops:
  0.0 0.7 %pad_add_fusion.numbers = s32[2,128]{1,0:T(2,128)S(1)} fusion(s32[1,128]{1,0:T(1,128)} %bitcast.6, s32[1,128]{1,0:T(1,128)} %bitcast.7), kind=kLoop, calls=%fused_computation | loop fusion | flops 256 | bytes 2048 | tf_op jit(solution)/shard_map/concatenate | solution.py:440
  0.7 50.5 %shard_map.46 = f32[16,128,128]{2,1,0:T(8,128)S(1)} custom-call(f32[16,8,16,128]{3,2,1,0:T(8,128)} %state.1, bf16[128,512,128]{2,1,0:T(8,128)(2,1)} %bitcast.5, s32[2,128]{1,0:T(2,128)S(1)} %pad_add_fusion.numbers), custom_call_target="tpu_custom_call" | custom-call | flops 268435456 | bytes 20971520 | tf_op jit(solution)/shard_map/pallas_call | solution.py:401
  51.2 1.0 %copy.6 = f32[16,8,16,128]{3,2,1,0:T(8,128)} copy(f32[16,8,16,128]{3,2,1,0:T(8,128)S(1)} %bitcast.4) | data formatting | bytes 2097152

commit v5 on v4

--- a/solution.py
+++ b/solution.py
@@ -11,13 +11,13 @@
 BF16 = jnp.bfloat16
 CHUNKS = 4
 STEPS = 128 // CHUNKS
-HALO_Z, HALO, META_LINE, META_PLANE, RIM, SPEED_CORE, SPEED_CHIPS, DELIVERY = range(8)
+HALO_Z, HALO_X, HALO_Y, META_LINE, META_PLANE, RIM, SPEED_CORE, SPEED_CHIPS, DELIVERY = range(9)
 
 
 def far_first():
     draws = np.random.RandomState(0).permutation(128)
     cells = [(int(t) // 32, int(t) // 8 % 4, int(t) % 8) for t in draws if t]
-    cells.sort(key=lambda o: -(min(o[0], 4 - o[0]) + min(o[1], 4 - o[1]) + min(o[2], 8 - o[2]) / 2))
+    cells.sort(key=lambda o: -(min(o[0], 4 - o[0]) + min(o[1], 4 - o[1]) + (min(o[2], 8 - o[2]) + 1) // 2))
     order = []
     for a, b, c in cells:
         for offset in ((a, b, c), (-a % 4, -b % 4, -c % 8)):
@@ -85,6 +85,8 @@
         greet(barrier, at(0, 0, c))
 
     load_state.wait()
+    for x in (1, 2, 3):
+        load_weights(x).start()
     lane16 = lax.broadcasted_iota(jnp.int32, (16, 128), 1)
 
     def to_blocks(x, carry):
@@ -110,11 +112,11 @@
     cells = pl.ds(1, 8)
     remote(zsend.at[1], zrecv.at[0], HALO_Z, at(0, 0, 1)).start()
     remote(zsend.at[0], zrecv.at[1], HALO_Z, at(0, 0, -1)).start()
-    remote(pad.at[8, inner], pad.at[0, inner], HALO, at(1, 0, 0)).start()
-    remote(pad.at[1, inner], pad.at[9, inner], HALO, at(-1, 0, 0)).start()
-    remote(pad.at[cells, 16], pad.at[cells, 0], HALO, at(0, 1, 0)).start()
-    remote(pad.at[cells, 1], pad.at[cells, 17], HALO, at(0, -1, 0)).start()
-    for x in (1, 2, 3, 4, 5, 6, 0, 7):
+    remote(pad.at[8, inner], pad.at[0, inner], HALO_X, at(1, 0, 0)).start()
+    remote(pad.at[1, inner], pad.at[9, inner], HALO_X, at(-1, 0, 0)).start()
+    remote(pad.at[cells, 16], pad.at[cells, 0], HALO_Y, at(0, 1, 0)).start()
+    remote(pad.at[cells, 1], pad.at[cells, 17], HALO_Y, at(0, -1, 0)).start()
+    for x in (4, 5, 6, 0, 7):
         load_weights(x).start()
 
     for a, b in plane[1:]:
@@ -159,15 +161,7 @@
     fetch_slots = pltpu.make_async_copy(slotv, slots, slot_sem.at[0])
     fetch_slots.start()
     contrib[128] = jnp.zeros((16, 128), F32)
-    received(pad.at[0:3, inner], HALO)
-
-    @pl.when(gx == 0)
-    def _():
-        pad[0, 1:17] = jnp.zeros((16, 16, 128), F32)
-
-    @pl.when(gx == 3)
-    def _():
-        pad[9, 1:17] = jnp.zeros((16, 16, 128), F32)
+    received(pad.at[0, inner], HALO_Y)
 
     @pl.when(gy == 0)
     def _():
@@ -183,6 +177,16 @@
         return carry
 
     lax.fori_loop(2, 8, side_columns, 0)
+    received(pad.at[0:2, inner], HALO_X)
+
+    @pl.when(gx == 0)
+    def _():
+        pad[0, 1:17] = jnp.zeros((16, 16, 128), F32)
+
+    @pl.when(gx == 3)
+    def _():
+        pad[9, 1:17] = jnp.zeros((16, 16, 128), F32)
+
     load_weights(0).wait()
     load_weights(7).wait()
 
@@ -386,7 +390,8 @@
     for x in range(8):
         advance(x)
     delivered(zsend, HALO_Z)
-    delivered(pad.at[0:3, inner], HALO)
+    delivered(pad.at[0:2, inner], HALO_X)
+    delivered(pad.at[0, inner], HALO_Y)
     delivered(meta.at[0, 1:8], META_LINE)
     delivered(meta.at[1:16], META_PLANE)
     delivered(sendbuf.at[0:127], DELIVERY)
@@ -428,7 +433,7 @@
             pltpu.VMEM((2, 8, 128), F32),
             pltpu.VMEM((64, 1, 128), F32),
             pltpu.SemaphoreType.REGULAR,
-            dma((8,)), dma((1,)), dma((1,)), dma((8,)), dma((7 + CHUNKS,)),
+            dma((8,)), dma((1,)), dma((1,)), dma((9,)), dma((8 + CHUNKS,)),
         ],
         compiler_params=pltpu.CompilerParams(
             collective_id=0, has_side_effects=True, vmem_limit_bytes=52 * 2**20

time: 52.3 us -> 51.7 us (0.989)
  Pallas kernels: 50.5 us -> 49.9 us
    pallas_call x1, Pallas kernels: 50.5 us -> 49.9 us  [on_device(): pl.pallas_call(kernel, out_shape=jax.ShapeDtypeStruct((16, 128, 128), F32...]
where the time goes in v5:
time: 51.7 us; the launch traced here: 51.5 us
  Pallas kernels  49.9 us (97%)
  local copies, waits for them, and re-layouts  0.97 us (2%)
  other arithmetic  0.68 us (1%)
    pallas_call x1, Pallas kernels, on_device(): pl.pallas_call(kernel, out_shape=jax.ShapeDtypeStruct((16, 128, 128), F32...  49.9 us

profile of v5, /device:TPU:1, one launch (start us, length us, event | category | flops | bytes accessed | tf_op | source)
XLA Modules:
  0.0 51.5 jit_solution(8688355431560022895)
XLA Ops:
  0.0 0.7 %pad_add_fusion.numbers = s32[2,128]{1,0:T(2,128)S(1)} fusion(s32[1,128]{1,0:T(1,128)} %bitcast.6, s32[1,128]{1,0:T(1,128)} %bitcast.7), kind=kLoop, calls=%fused_computation | loop fusion | flops 256 | bytes 2048 | tf_op jit(solution)/shard_map/concatenate | solution.py:445
  0.7 49.9 %shard_map.46 = f32[16,128,128]{2,1,0:T(8,128)S(1)} custom-call(f32[16,8,16,128]{3,2,1,0:T(8,128)} %state.1, bf16[128,512,128]{2,1,0:T(8,128)(2,1)} %bitcast.5, s32[2,128]{1,0:T(2,128)S(1)} %pad_add_fusion.numbers), custom_call_target="tpu_custom_call" | custom-call | flops 268435456 | bytes 20971520 | tf_op jit(solution)/shard_map/pallas_call | solution.py:406
  50.6 1.0 %copy.6 = f32[16,8,16,128]{3,2,1,0:T(8,128)} copy(f32[16,8,16,128]{3,2,1,0:T(8,128)S(1)} %bitcast.4) | data formatting | bytes 2097152

commit v6 on v5

--- a/solution.py
+++ b/solution.py
@@ -234,22 +234,32 @@
         both = jnp.concatenate([hot_0[rows], hot_1[rows], hot_0[rows], hot_1[rows]], axis=0)
         lhs[chunk] = both.T.astype(BF16)
 
+    def arrange(chunk, half):
+        for part in range(STEPS // 16):
+            for slot in range(2):
+                tile = recvbuf[pl.ds(chunk * STEPS + part * 16, 16), slot, pl.ds(half * 8, 8), :]
+                tile = jnp.swapaxes(tile, 0, 1)
+                upper = tile.astype(BF16)
+                lower = (tile - upper.astype(F32)).astype(BF16)
+                row = slot * STEPS + part * 16
+                rhs[pl.ds(half * 8, 8), pl.ds(row, 16), :] = upper
+                rhs[pl.ds(half * 8, 8), pl.ds(2 * STEPS + row, 16), :] = lower
+
+    def accumulate(chunk, which):
+        for f in which:
+            part_sum = jnp.dot(lhs[chunk], rhs[f], preferred_element_type=F32)
+            fields[f] = part_sum if chunk == 0 else fields[f] + part_sum
+
+    final = CHUNKS - 1
     for chunk in range(CHUNKS):
         start = chunk * STEPS
         received(recvbuf.at[start : min(start + STEPS, 127)], DELIVERY, chunk)
-        for part in range(STEPS // 16):
-            for slot in range(2):
-                for half in range(2):
-                    tile = recvbuf[pl.ds(start + part * 16, 16), slot, pl.ds(half * 8, 8), :]
-                    tile = jnp.swapaxes(tile, 0, 1)
-                    upper = tile.astype(BF16)
-                    lower = (tile - upper.astype(F32)).astype(BF16)
-                    row = slot * STEPS + part * 16
-                    rhs[pl.ds(half * 8, 8), pl.ds(row, 16), :] = upper
-                    rhs[pl.ds(half * 8, 8), pl.ds(2 * STEPS + row, 16), :] = lower
-        for f in range(16):
-            part_sum = jnp.dot(lhs[chunk], rhs[f], preferred_element_type=F32)
-            fields[f] = part_sum if chunk == 0 else fields[f] + part_sum
+        arrange(chunk, 0)
+        if chunk < final:
+            arrange(chunk, 1)
+            accumulate(chunk, range(16))
+        else:
+            accumulate(chunk, range(5))
 
     square = fields[4] * fields[4] + (fields[1] * fields[1] + fields[2] * fields[2] + fields[3] * fields[3])
     own_core = lax.rem(gz, 2)
@@ -294,6 +304,9 @@
     chips = [offset for offset in OFFSETS if offset[2] % 2 == 0]
     for k, offset in enumerate(chips[:63]):
         remote(max2.at[0], max2.at[k + 1], SPEED_CHIPS, at(*offset)).start()
+
+    arrange(final, 1)
+    accumulate(final, range(5, 16))
 
     received(contrib.at[0:38], RIM)
     sub8 = lax.broadcasted_iota(jnp.int32, (8, 128), 0)

time: 51.7 us -> 51.5 us (level)
  no operation moved by 1% of the time
where the time goes in v6:
time: 51.5 us; the launch traced here: 51.4 us
  Pallas kernels  49.7 us (97%)
  local copies, waits for them, and re-layouts  0.97 us (2%)
  other arithmetic  0.68 us (1%)
    pallas_call x1, Pallas kernels, on_device(): pl.pallas_call(kernel, out_shape=jax.ShapeDtypeStruct((16, 128, 128), F32...  49.7 us

profile of v6, /device:TPU:1, one launch (start us, length us, event | category | flops | bytes accessed | tf_op | source)
XLA Modules:
  0.0 51.4 jit_solution(6511479382956553451)
XLA Ops:
  0.0 0.7 %pad_add_fusion.numbers = s32[2,128]{1,0:T(2,128)S(1)} fusion(s32[1,128]{1,0:T(1,128)} %bitcast.6, s32[1,128]{1,0:T(1,128)} %bitcast.7), kind=kLoop, calls=%fused_computation | loop fusion | flops 256 | bytes 2048 | tf_op jit(solution)/shard_map/concatenate | solution.py:458
  0.7 49.7 %shard_map.46 = f32[16,128,128]{2,1,0:T(8,128)S(1)} custom-call(f32[16,8,16,128]{3,2,1,0:T(8,128)} %state.1, bf16[128,512,128]{2,1,0:T(8,128)(2,1)} %bitcast.5, s32[2,128]{1,0:T(2,128)S(1)} %pad_add_fusion.numbers), custom_call_target="tpu_custom_call" | custom-call | flops 268435456 | bytes 20971520 | tf_op jit(solution)/shard_map/pallas_call | solution.py:419
  50.4 1.0 %copy.6 = f32[16,8,16,128]{3,2,1,0:T(8,128)} copy(f32[16,8,16,128]{3,2,1,0:T(8,128)S(1)} %bitcast.4) | data formatting | bytes 2097152
